TPU v7x, 32 devices: a whole 2x2x4 slice. The times are simulated.
32 devices in a mesh: gx: 8 (over z, y), gy: 4 (over x, core).
Axes of the slice: x: 2, y: 2, z: 4, core: 2. Of those that a mesh axis runs over, the one named last changes fastest.
Arguments:
- prec_pops: float32 [27, 32, 32, 256], P(None, 'gx', 'gy'), may hold values from 0 to 1, as said below
- main_pops: float32 [27, 64, 64, 256], P(None, 'gx', 'gy'), may hold values from 0 to 1, as said below
- cell_type: int32 [64, 64, 256], P('gx', 'gy'), may hold values from 0 to 2, as said below
- rates: float32 [27], replicated, may hold values from 0.7 to 1.8
Outputs:
- prec_next: float32 [27, 32, 32, 256], P(None, 'gx', 'gy')
- main_next: float32 [27, 64, 64, 256], P(None, 'gx', 'gy')
Inputs may be any that keep to these rules, and one draw needn't show every extreme that they name: `prec_pops`: every population is positive; the populations of a cell sum to between 0.6 and 1.5. `main_pops`: every population is positive; the populations of a cell sum to between 0.6 and 1.5. `cell_type`: the lowest one to three cells of every column are solid (1); above them cells are fluid (0) or turbine disk (2).
All inputs are finite; a program needn't handle non-finite values.
Results may differ from a plain program's by a relative error of at most 0.000076.
Values sent between devices are 32-bit elements; how exact they have to be, the bound alone decides.
No kernel may reach another device: no remote copies, remote signals or barrier semaphores. Data moves between devices by JAX's collectives and lax.ppermute only.
A program may use at most 128 MiB of HBM per device.

v0:
```python
import jax
import jax.numpy as jnp
import numpy as np
from jax import lax
from jax.experimental import pallas as pl
from jax.experimental.pallas import tpu as pltpu
from jax.sharding import PartitionSpec as P

drag_scale = -0.5 * 0.75
vmem_bytes = 56 * 1024 * 1024
any_space = pl.BlockSpec(memory_space=pl.ANY)
vmem_space = pl.BlockSpec(memory_space=pltpu.VMEM)
smem_space = pl.BlockSpec(memory_space=pltpu.SMEM)


def swap_pairs(count, first):
    pairs = [(i, (i + 1) % count) for i in range(first, count, 2)]
    return [p for a, b in pairs for p in ((a, b), (b, a))]


def along_axes(values, stride, step):
    out = list(values)
    for start in range(27):
        if (start // stride) % 3 == 0:
            where = (start, start + stride, start + 2 * stride)
            for place, value in zip(where, step(*(values[i] for i in where))):
                out[place] = value
    return out


def to_moments(low, mid, high):
    outer = low + high
    return outer + mid, high - low, outer


def from_moments(zeroth, first, second):
    low, high = second - first, second + first
    return low, zeroth - (low + high), high


def digits(k):
    return k // 9, k // 3 % 3, k % 3


def moment_scales(rates_ref):
    keep, pull = [], []
    for k in range(27):
        ones = digits(k).count(1)
        twos = digits(k).count(2)
        half = 0.5 ** (ones + twos)
        third = 3.0 ** -(twos if ones else max(twos - 1, 0))
        rate = rates_ref[k]
        keep.append((1.0 - rate) * half)
        pull.append(rate * (half * third))
    return keep, pull


def relaxed_tile(pops, keep, pull, disk):
    m = pops
    for stride in (1, 3, 9):
        m = along_axes(m, stride, to_moments)
    density, flux = m[0], (m[9], m[3], m[1])
    inverse = 1.0 / density
    speed = [f * inverse for f in flux]
    third = density * (1.0 / 3.0)
    product = {(a, b): flux[a] * speed[b] for a in range(3) for b in range(a, 3)}
    drag = None
    if disk is not None:
        drag = jnp.where(disk, drag_scale * flux[0] * jnp.abs(speed[0]), 0.0)
    target = []
    for k in range(27):
        ones = [a for a in range(3) if digits(k)[a] == 1]
        twos = [a for a in range(3) if digits(k)[a] == 2]
        half = 0.5 ** (len(ones) + len(twos))
        if not ones and not twos:
            value = density
        elif len(ones) == 1 and not twos:
            value = m[k] * half
        elif len(ones) == 3:
            value = m[k] * keep[k]
        else:
            if len(ones) == 1:
                pulled = flux[ones[0]]
            elif len(ones) == 2:
                pulled = product[tuple(ones)]
            else:
                pulled = third
                for a in twos:
                    pulled = pulled + product[a, a]
            value = m[k] * keep[k] + pulled * pull[k]
        if drag is not None and ones == [0]:
            value = value + drag * (half * 3.0 ** -len(twos))
        target.append(value)
    for stride in (9, 3, 1):
        target = along_axes(target, stride, from_moments)
    return target


def collide_kernel(
    main_hbm, prec_hbm, cells_hbm, rates_ref,
    rel_main, rel_prec, send_a, send_b, send_c, send_d,
    main_in, prec_in, cells_in, side_low, side_high, in_sem, cell_sem, out_sem,
):
    extent_x, extent_y, depth = main_in.shape[1:]
    prec_x, prec_y = prec_in.shape[1:3]
    odd_x = lax.rem(lax.axis_index("gx"), 2)
    odd_y = lax.rem(lax.axis_index("gy"), 2)

    def fetch_main(x):
        return pltpu.make_async_copy(main_hbm.at[:, x], main_in.at[:, x], in_sem.at[x])

    def fetch_prec(x):
        return pltpu.make_async_copy(
            prec_hbm.at[:, x], prec_in.at[:, x], in_sem.at[extent_x + x]
        )

    fetch_cells = pltpu.make_async_copy(cells_hbm, cells_in, cell_sem)
    for x in range(prec_x):
        fetch_prec(x).start()
    fetch_cells.start()
    for x in range(extent_x):
        fetch_main(x).start()
    keep, pull = moment_scales(rates_ref)

    def prec_plane(x, carry):
        fetch_prec(x).wait()
        for y in range(0, prec_y, 8):
            for z in range(0, depth, 128):
                rows, lanes = pl.ds(y, 8), pl.ds(z, 128)
                pops = [prec_in[i, x, rows, lanes] for i in range(27)]
                for i, value in enumerate(relaxed_tile(pops, keep, pull, None)):
                    rel_prec[i, x, rows, lanes] = value
        return carry

    def main_plane(x, carry):
        fetch_main(x).wait()
        for y in range(0, extent_y, 8):
            for z in range(0, depth, 128):
                rows, lanes = pl.ds(y, 8), pl.ds(z, 128)
                kind = cells_in[x, rows, lanes]
                pops = [main_in[i, x, rows, lanes] for i in range(27)]
                for i, value in enumerate(relaxed_tile(pops, keep, pull, kind == 2)):
                    if z == 0:
                        value = jnp.where(kind == 1, main_in[26 - i, x, rows, lanes], value)
                    rel_main[i, x, rows, lanes] = value
        return carry

    lax.fori_loop(0, prec_x, prec_plane, 0)
    fetch_cells.wait()
    lax.fori_loop(0, extent_x, main_plane, 0)

    planes = extent_x + prec_x
    for pair in range(9):
        down, up = 9 * (pair // 3) + pair % 3, 9 * (pair // 3) + 6 + pair % 3
        for x in range(extent_x):
            place = pl.ds(pair * planes + x, 1)
            side_low[place, :] = rel_main[down, x, 0:1, :]
            side_high[place, :] = rel_main[up, x, extent_y - 1 : extent_y, :]
        for x in range(prec_x):
            place = pl.ds(pair * planes + extent_x + x, 1)
            side_low[place, :] = rel_prec[down, x, 0:1, :]
            side_high[place, :] = rel_prec[up, x, prec_y - 1 : prec_y, :]

    main_rows, prec_rows = pl.ds(0, extent_y), pl.ds(extent_y, prec_y)

    def faces(high_to, low_to):
        return (
            pltpu.make_async_copy(
                rel_main.at[18:27, extent_x - 1], high_to.at[:, main_rows], out_sem.at[0]
            ),
            pltpu.make_async_copy(
                rel_prec.at[18:27, prec_x - 1], high_to.at[:, prec_rows], out_sem.at[1]
            ),
            pltpu.make_async_copy(rel_main.at[0:9, 0], low_to.at[:, main_rows], out_sem.at[2]),
            pltpu.make_async_copy(rel_prec.at[0:9, 0], low_to.at[:, prec_rows], out_sem.at[3]),
        )

    def sides(high_to, low_to):
        return (
            pltpu.make_async_copy(side_high, high_to, out_sem.at[4]),
            pltpu.make_async_copy(side_low, low_to, out_sem.at[5]),
        )

    def both(odd, copies, one, other):
        @pl.when(odd == 0)
        def even_place():
            for copy in copies(one, other):
                copy.start()

        @pl.when(odd == 1)
        def odd_place():
            for copy in copies(other, one):
                copy.start()

    both(odd_x, faces, send_a, send_b)
    both(odd_y, sides, send_c, send_d)
    for copy in faces(send_a, send_b) + sides(send_c, send_d):
        copy.wait()


def corner_kernel(rel_prec, recv_c, recv_d, corner_a, corner_b, inlet_send, low_v, high_v, sem):
    prec_x, prec_y = rel_prec.shape[1:3]
    planes = recv_c.shape[0] // 9
    extent_x = planes - prec_x
    odd_x = lax.rem(lax.axis_index("gx"), 2)
    odd_y = lax.rem(lax.axis_index("gy"), 2)

    def from_sides(low_from, high_from):
        return (
            pltpu.make_async_copy(low_from, low_v, sem.at[0]),
            pltpu.make_async_copy(high_from, high_v, sem.at[1]),
        )

    @pl.when(odd_y == 0)
    def even_side():
        for copy in from_sides(recv_d, recv_c):
            copy.start()

    @pl.when(odd_y == 1)
    def odd_side():
        for copy in from_sides(recv_c, recv_d):
            copy.start()

    for copy in from_sides(recv_d, recv_c):
        copy.wait()

    def corners(ref, first, x_main, x_prec):
        for lattice, x in enumerate((x_main, extent_x + x_prec)):
            for step in range(3):
                place = pl.ds((first + step) * planes + x, 1)
                ref[lattice, step : step + 1, :] = low_v[place, :]
                ref[lattice, 3 + step : 4 + step, :] = high_v[place, :]

    corner_a[...] = jnp.zeros_like(corner_a)
    corner_b[...] = jnp.zeros_like(corner_b)

    @pl.when(odd_x == 0)
    def even_corner():
        corners(corner_a, 6, extent_x - 1, prec_x - 1)
        corners(corner_b, 0, 0, 0)

    @pl.when(odd_x == 1)
    def odd_corner():
        corners(corner_b, 6, extent_x - 1, prec_x - 1)
        corners(corner_a, 0, 0, 0)

    inlet_send[0:9] = rel_prec[18:27, prec_x - 1]
    inlet_send[9] = jnp.zeros(inlet_send.shape[1:], jnp.float32)

    @pl.when(odd_y == 0)
    def even_inlet():
        for step in range(3):
            place = pl.ds((6 + step) * planes + extent_x + prec_x - 1, 1)
            inlet_send[9, step : step + 1, :] = low_v[place, :]

    @pl.when(odd_y == 1)
    def odd_inlet():
        for step in range(3):
            place = pl.ds((6 + step) * planes + extent_x + prec_x - 1, 1)
            inlet_send[9, step : step + 1, :] = high_v[place, :]


def stream_kernel(
    rel_main, rel_prec, recv_a, recv_b, recv_c, recv_d, corner_a, corner_b, inlet_a, inlet_b,
    main_out, prec_out,
    main_v, prec_v, face_low, face_high, side_low, side_high, corner_low, corner_high, sem, out_sem,
):
    extent_x, extent_y, depth = rel_main.shape[1:]
    prec_x, prec_y = rel_prec.shape[1:3]
    planes = extent_x + prec_x
    place_x, place_y = lax.axis_index("gx"), lax.axis_index("gy")
    count_x, count_y = lax.axis_size("gx"), lax.axis_size("gy")
    odd_x, odd_y = lax.rem(place_x, 2), lax.rem(place_y, 2)

    def bring(low_from, high_from, low_to, high_to, first):
        return (
            pltpu.make_async_copy(low_from, low_to, sem.at[first]),
            pltpu.make_async_copy(high_from, high_to, sem.at[first + 1]),
        )

    groups = (
        (odd_x, recv_a, recv_b, face_low, face_high, 0),
        (odd_y, recv_c, recv_d, side_low, side_high, 2),
        (odd_x, corner_a, corner_b, corner_low, corner_high, 4),
    )
    for odd, one, other, low_to, high_to, first in groups:

        @pl.when(odd == 0)
        def even_place():
            for copy in bring(other, one, low_to, high_to, first):
                copy.start()

        @pl.when(odd == 1)
        def odd_place():
            for copy in bring(one, other, low_to, high_to, first):
                copy.start()

    for odd, one, other, low_to, high_to, first in groups:
        for copy in bring(other, one, low_to, high_to, first):
            copy.wait()

    def inlet(lower, upper):
        face_low[:, 0:prec_y] = lower[0:9]
        face_low[:, prec_y : 2 * prec_y] = upper[0:9]
        corner_low[0, 0:3] = lower[9, 0:3]
        corner_low[0, 3:6] = upper[9, 0:3]

    @pl.when((place_x == 0) & (place_y < count_y // 2))
    def near_inlet():
        inlet(inlet_a, inlet_b)

    @pl.when((place_x == 0) & (place_y >= count_y // 2))
    def far_inlet():
        inlet(inlet_b, inlet_a)

    @pl.when(place_x == count_x - 1)
    def outlet():
        face_high[:, 0:extent_y] = rel_main[0:9, extent_x - 1]
        for step in range(3):
            place = pl.ds(step * planes + extent_x - 1, 1)
            corner_high[0, step : step + 1, :] = side_low[place, :]
            corner_high[0, 3 + step : 4 + step, :] = side_high[place, :]

    def plane(x, rel, out, lattice, edge):
        size_x, size_y = rel.shape[1:3]
        start_y, start_x = (extent_y, extent_x) if lattice else (0, 0)
        row = lax.broadcasted_iota(jnp.int32, (size_y, depth), 0)
        lane = lax.broadcasted_iota(jnp.int32, (size_y, depth), 1)
        for i in range(27):
            step_x, step_y, step_z = (d - 1 for d in digits(i))
            pair = 3 * (step_x + 1) + step_z + 1
            source = x - step_x
            outside = None
            if edge == "first" and step_x == 1:
                outside = face_low, corner_low
            elif edge == "last" and step_x == -1:
                outside = face_high, corner_high
            if outside is not None:
                value = outside[0][3 * (step_y + 1) + step_z + 1, pl.ds(start_y, size_y), :]
            else:
                value = rel[i, source]
            if step_y:
                if outside is not None:
                    where = (0 if step_y == 1 else 3) + step_z + 1
                    halo = outside[1][lattice, where : where + 1, :]
                else:
                    side = side_low if step_y == 1 else side_high
                    halo = side[pl.ds(pair * planes + start_x + source, 1), :]
                value = pltpu.roll(value, 1 if step_y == 1 else size_y - 1, 0)
                value = jnp.where(row == (0 if step_y == 1 else size_y - 1), halo, value)
            if step_z:
                value = pltpu.roll(value, 1 if step_z == 1 else depth - 1, 1)
                value = jnp.where(
                    lane == (0 if step_z == 1 else depth - 1), rel[26 - i, x], value
                )
            out[i, x] = value

    def put(out_v, out_hbm, x, which):
        return pltpu.make_async_copy(out_v.at[:, x], out_hbm.at[:, x], out_sem.at[which])

    for rel, out_v, out_hbm, lattice in (
        (rel_main, main_v, main_out, 0),
        (rel_prec, prec_v, prec_out, 1),
    ):
        size_x = rel.shape[1]
        first = 0 if lattice == 0 else extent_x

        def inner(x, carry):
            plane(x, rel, out_v, lattice, "")
            put(out_v, out_hbm, x, first + x).start()
            return carry

        lax.fori_loop(1, size_x - 1, inner, 0)
        for x, edge in ((0, "first"), (size_x - 1, "last")):
            plane(x, rel, out_v, lattice, edge)
            put(out_v, out_hbm, x, first + x).start()
    for x in range(extent_x):
        put(main_v, main_out, x, x).wait()
    for x in range(prec_x):
        put(prec_v, prec_out, x, extent_x + x).wait()


def shards(prec_pops, main_pops, cell_type, rates):
    _, extent_x, extent_y, depth = main_pops.shape
    _, prec_x, prec_y, _ = prec_pops.shape
    count_x, count_y = lax.axis_size("gx"), lax.axis_size("gy")
    assert count_x % 2 == 0 and count_y % 2 == 0 and extent_y == 2 * prec_y
    planes = extent_x + prec_x
    f32 = jnp.float32
    face = jax.ShapeDtypeStruct((9, extent_y + prec_y, depth), f32)
    side = jax.ShapeDtypeStruct((9 * planes, depth), f32)
    params = pltpu.CompilerParams(vmem_limit_bytes=vmem_bytes)
    dma = pltpu.SemaphoreType.DMA
    main_rel, prec_rel, send_a, send_b, send_c, send_d = pl.pallas_call(
        collide_kernel,
        out_shape=(
            jax.ShapeDtypeStruct(main_pops.shape, f32),
            jax.ShapeDtypeStruct(prec_pops.shape, f32),
            face, face, side, side,
        ),
        in_specs=[any_space] * 3 + [smem_space],
        out_specs=(vmem_space, vmem_space) + (any_space,) * 4,
        scratch_shapes=[
            pltpu.VMEM(main_pops.shape, f32),
            pltpu.VMEM(prec_pops.shape, f32),
            pltpu.VMEM(cell_type.shape, jnp.int32),
            pltpu.VMEM(side.shape, f32),
            pltpu.VMEM(side.shape, f32),
            dma((planes,)), dma(()), dma((6,)),
        ],
        compiler_params=params,
        name="collide",
    )(main_pops, prec_pops, cell_type, rates)

    recv_c = lax.ppermute(send_c, "gy", swap_pairs(count_y, 0))
    recv_d = lax.ppermute(send_d, "gy", swap_pairs(count_y, 1))
    recv_a = lax.ppermute(send_a, "gx", swap_pairs(count_x, 0))
    recv_b = lax.ppermute(send_b, "gx", swap_pairs(count_x, 1))

    corner = jax.ShapeDtypeStruct((2, 8, depth), f32)
    corner_a, corner_b, inlet_send = pl.pallas_call(
        corner_kernel,
        out_shape=(corner, corner, jax.ShapeDtypeStruct((10, prec_y, depth), f32)),
        in_specs=[vmem_space, any_space, any_space],
        out_specs=(vmem_space,) * 3,
        scratch_shapes=[pltpu.VMEM(side.shape, f32), pltpu.VMEM(side.shape, f32), dma((2,))],
        compiler_params=params,
        name="corners",
    )(prec_rel, recv_c, recv_d)

    half = count_y // 2
    base = (count_x - 1) * count_y
    near = [(base + s, s // 2 + half * (s % 2)) for s in range(count_y)]
    far = [(base + s, s // 2 + half * (1 - s % 2)) for s in range(count_y)]
    corner_a = lax.ppermute(corner_a, "gx", swap_pairs(count_x, 0))
    corner_b = lax.ppermute(corner_b, "gx", swap_pairs(count_x, 1))
    inlet_a = lax.ppermute(inlet_send, ("gx", "gy"), near)
    inlet_b = lax.ppermute(inlet_send, ("gx", "gy"), far)

    main_next, prec_next = pl.pallas_call(
        stream_kernel,
        out_shape=(
            jax.ShapeDtypeStruct(main_pops.shape, f32),
            jax.ShapeDtypeStruct(prec_pops.shape, f32),
        ),
        in_specs=[vmem_space] * 2 + [any_space] * 6 + [vmem_space] * 2,
        out_specs=(any_space, any_space),
        scratch_shapes=[
            pltpu.VMEM(main_pops.shape, f32),
            pltpu.VMEM(prec_pops.shape, f32),
            pltpu.VMEM(face.shape, f32),
            pltpu.VMEM(face.shape, f32),
            pltpu.VMEM(side.shape, f32),
            pltpu.VMEM(side.shape, f32),
            pltpu.VMEM(corner.shape, f32),
            pltpu.VMEM(corner.shape, f32),
            dma((6,)), dma((planes,)),
        ],
        compiler_params=params,
        name="stream",
    )(
        main_rel, prec_rel, recv_a, recv_b, recv_c, recv_d,
        corner_a, corner_b, inlet_a, inlet_b,
    )
    return prec_next, main_next


def solution(mesh):
    placed = (P(None, "gx", "gy", None), P(None, "gx", "gy", None), P("gx", "gy", None), P())
    return jax.shard_map(
        shards,
        mesh=mesh,
        in_specs=placed,
        out_specs=(P(None, "gx", "gy", None), P(None, "gx", "gy", None)),
        check_vma=False,
    )
```

profile of v0, /device:TPU:0, one launch (start us, length us, event | category | flops | bytes accessed | tf_op | source)
XLA Modules:
  0.0 44.8 jit_solution(15905585904969030764)
XLA Ops:
  0.6 7.5 %collide.1 = (f32[27,8,16,256]{3,2,1,0:T(8,128)}, f32[27,4,8,256]{3,2,1,0:T(8,128)}, f32[9,24,256]{2,1,0:T(8,128)}, f32[9,24,256]{2,1,0:T(8,128)}, f32[108,256]{1,0:T(8,128)}, /*index=5*/f32[108,256]{1,0:T(8,128)}) custom-call(f32[27,8,16,256]{3,2,1,0:T(8,128)} %main_hbm.1, f32[27,4,8,256]{3,2,1,0:T(8,128)} %prec_hbm.1, s32[8,16,256]{2,1,0:T(8,128)} %cells_hbm.1, ...), custom_call_target="tpu_custom_call" | custom-call | tf_op jit(solution)/shard_map/collide/pallas_call | solution.py:394
  8.2 3.0 %collective-permute-start = (f32[9,24,256]{2,1,0:T(8,128)}, f32[9,24,256]{2,1,0:T(8,128)S(1)}, u32[]{:S(2)}, u32[]{:S(2)}) collective-permute-start(f32[9,24,256]{2,1,0:T(8,128)} %get-tuple-element.15), channel_id=1, source_target_pairs={{0,4},{4,0},{8,12},{12,8},{16,20},{20,16},{24,28},{28,24},{1,5},{5... | collective-permute-start | bytes 663560 | tf_op jit(solution)/shard_map/ppermute | solution.py:417
  11.2 3.5 %collective-permute-start.1 = (f32[9,24,256]{2,1,0:T(8,128)}, f32[9,24,256]{2,1,0:T(8,128)S(1)}, u32[]{:S(2)}, u32[]{:S(2)}) collective-permute-start(f32[9,24,256]{2,1,0:T(8,128)} %get-tuple-element.16), channel_id=1, source_target_pairs={{4,8},{8,4},{12,16},{16,12},{20,24},{24,20},{28,0},{0,28},{5,9},{9... | collective-permute-start | bytes 663560 | tf_op jit(solution)/shard_map/ppermute | solution.py:418
  14.7 0.0 collective-permute-start.2
  14.8 1.6 %collective-permute-start.3 = (f32[108,256]{1,0:T(8,128)}, f32[108,256]{1,0:T(8,128)S(1)}, u32[]{:S(2)}, u32[]{:S(2)}) collective-permute-start(f32[108,256]{1,0:T(8,128)} %get-tuple-element.18), channel_id=1, source_target_pairs={{1,2},{2,1},{3,0},{0,3},{5,6},{6,5},{7,4},{4,7},{9,10},{10,9},{11,... | collective-permute-start | bytes 331784 | tf_op jit(solution)/shard_map/ppermute | solution.py:416
  16.4 0.0 collective-permute-done.2.recv_c
  16.4 3.4 %collective-permute-done.3.recv_d = f32[108,256]{1,0:T(8,128)S(1)} collective-permute-done((f32[108,256]{1,0:T(8,128)}, f32[108,256]{1,0:T(8,128)S(1)}, u32[]{:S(2)}, u32[]{:S(2)}) %collective-permute-start.3) | collective-permute-done | bytes 110624 | tf_op jit(solution)/shard_map/ppermute | solution.py:416
  19.8 0.0 copy-start.1
  19.8 0.0 copy-done
  19.8 0.6 %copy-done.1 = f32[108,256]{1,0:T(8,128)} copy-done((f32[108,256]{1,0:T(8,128)}, f32[108,256]{1,0:T(8,128)S(1)}, u32[]{:S(2)}) %copy-start.1) | copy-done | bytes 110616
  20.4 2.8 %corners.1 = (f32[2,8,256]{2,1,0:T(8,128)}, f32[2,8,256]{2,1,0:T(8,128)}, f32[10,8,256]{2,1,0:T(8,128)}) custom-call(f32[27,4,8,256]{3,2,1,0:T(8,128)} %get-tuple-element.14.rel_prec, f32[108,256]{1,0:T(8,128)} %copy-done, f32[108,256]{1,0:T(8,128)} %copy-done.1), custom_call_target="tpu_custom_call" | custom-call | tf_op jit(solution)/shard_map/corners/pallas_call | solution.py:421
  23.2 1.3 %collective-permute-start.7 = (f32[10,8,256]{2,1,0:T(8,128)}, f32[10,8,256]{2,1,0:T(8,128)S(1)}, u32[]{:S(2)}, u32[]{:S(2)}) collective-permute-start(f32[10,8,256]{2,1,0:T(8,128)} %get-tuple-element.21), channel_id=1, source_target_pairs={{28,2},{29,0},{30,3},{31,1}} | collective-permute-start | bytes 245768 | tf_op jit(solution)/shard_map/ppermute | solution.py:438
  24.5 1.3 %collective-permute-start.6 = (f32[10,8,256]{2,1,0:T(8,128)}, f32[10,8,256]{2,1,0:T(8,128)S(1)}, u32[]{:S(2)}, u32[]{:S(2)}) collective-permute-start(f32[10,8,256]{2,1,0:T(8,128)} %get-tuple-element.21), channel_id=1, source_target_pairs={{28,0},{29,2},{30,1},{31,3}} | collective-permute-start | bytes 245768 | tf_op jit(solution)/shard_map/ppermute | solution.py:437
  25.8 0.1 collective-permute-start.4
  25.9 3.9 %collective-permute-done.4.corner_a = f32[2,8,256]{2,1,0:T(8,128)S(1)} collective-permute-done((f32[2,8,256]{2,1,0:T(8,128)}, f32[2,8,256]{2,1,0:T(8,128)S(1)}, u32[]{:S(2)}, u32[]{:S(2)}) %collective-permute-start.4) | collective-permute-done | bytes 16416 | tf_op jit(solution)/shard_map/ppermute | solution.py:435
  29.8 0.0 copy-start.6
  29.8 6.3 %collective-permute-start.5 = (f32[2,8,256]{2,1,0:T(8,128)}, f32[2,8,256]{2,1,0:T(8,128)S(1)}, u32[]{:S(2)}, u32[]{:S(2)}) collective-permute-start(f32[2,8,256]{2,1,0:T(8,128)} %get-tuple-element.20), channel_id=1, source_target_pairs={{4,8},{8,4},{12,16},{16,12},{20,24},{24,20},{28,0},{0,28},{5,9},{9... | collective-permute-start | bytes 49160 | tf_op jit(solution)/shard_map/ppermute | solution.py:436
  36.1 1.9 %collective-permute-done.5.corner_b = f32[2,8,256]{2,1,0:T(8,128)S(1)} collective-permute-done((f32[2,8,256]{2,1,0:T(8,128)}, f32[2,8,256]{2,1,0:T(8,128)S(1)}, u32[]{:S(2)}, u32[]{:S(2)}) %collective-permute-start.5) | collective-permute-done | bytes 16416 | tf_op jit(solution)/shard_map/ppermute | solution.py:436
  38.0 0.0 collective-permute-done.7.inlet_b
  38.0 0.0 collective-permute-done.6.inlet_a
  38.1 0.0 copy-start.5
  38.1 0.0 collective-permute-done.recv_a
  38.1 0.0 copy-start.2
  38.1 0.0 collective-permute-done.1.recv_b
  38.1 0.0 copy-start.3
  38.1 0.0 copy-done.6
  38.1 0.5 %copy-done.7 = f32[2,8,256]{2,1,0:T(8,128)} copy-done((f32[2,8,256]{2,1,0:T(8,128)}, f32[2,8,256]{2,1,0:T(8,128)S(1)}, u32[]{:S(2)}) %copy-start.7) | copy-done | bytes 16408
  38.6 0.0 copy-done.4
  38.7 0.0 copy-done.5
  38.7 0.1 copy-done.2
  38.8 0.1 copy-done.3
  38.9 5.9 %stream.1 = (f32[27,8,16,256]{3,2,1,0:T(8,128)}, f32[27,4,8,256]{3,2,1,0:T(8,128)}) custom-call(f32[27,8,16,256]{3,2,1,0:T(8,128)} %get-tuple-element.13.rel_main, f32[27,4,8,256]{3,2,1,0:T(8,128)} %get-tuple-element.14.rel_prec, f32[9,24,256]{2,1,0:T(8,128)} %copy-done.2, f32[9,24,256]{2,1,0:T(8,128)} %copy-done.3, f32[108,256]{1,0:T(8,128)} %copy-done, ...), custom_call_target="tpu_custom_call" | custom-call | tf_op jit(solution)/shard_map/stream/pallas_call | solution.py:440
  (3 shorter events, 0.0 us)
Async XLA Ops:
  8.2 29.9 %collective-permute-start = (f32[9,24,256]{2,1,0:T(8,128)}, f32[9,24,256]{2,1,0:T(8,128)S(1)}, u32[]{:S(2)}, u32[]{:S(2)}) collective-permute-start(f32[9,24,256]{2,1,0:T(8,128)} %get-tuple-element.15), channel_id=1, source_target_pairs={{0,4},{4,0},{8,12},{12,8},{16,20},{20,16},{24,28},{28,24},{1,5},{5... | collective-permute-start | bytes 663560 | tf_op jit(solution)/shard_map/ppermute | solution.py:417
  11.2 26.9 %collective-permute-start.1 = (f32[9,24,256]{2,1,0:T(8,128)}, f32[9,24,256]{2,1,0:T(8,128)S(1)}, u32[]{:S(2)}, u32[]{:S(2)}) collective-permute-start(f32[9,24,256]{2,1,0:T(8,128)} %get-tuple-element.16), channel_id=1, source_target_pairs={{4,8},{8,4},{12,16},{16,12},{20,24},{24,20},{28,0},{0,28},{5,9},{9... | collective-permute-start | bytes 663560 | tf_op jit(solution)/shard_map/ppermute | solution.py:418
  14.7 1.6 %collective-permute-start.2 = (f32[108,256]{1,0:T(8,128)}, f32[108,256]{1,0:T(8,128)S(1)}, u32[]{:S(2)}, u32[]{:S(2)}) collective-permute-start(f32[108,256]{1,0:T(8,128)} %get-tuple-element.17), channel_id=1, source_target_pairs={{0,1},{1,0},{2,3},{3,2},{4,5},{5,4},{6,7},{7,6},{8,9},{9,8},{10,11... | collective-permute-start | bytes 331784 | tf_op jit(solution)/shard_map/ppermute | solution.py:415
  14.8 5.0 %collective-permute-start.3 = (f32[108,256]{1,0:T(8,128)}, f32[108,256]{1,0:T(8,128)S(1)}, u32[]{:S(2)}, u32[]{:S(2)}) collective-permute-start(f32[108,256]{1,0:T(8,128)} %get-tuple-element.18), channel_id=1, source_target_pairs={{1,2},{2,1},{3,0},{0,3},{5,6},{6,5},{7,4},{4,7},{9,10},{10,9},{11,... | collective-permute-start | bytes 331784 | tf_op jit(solution)/shard_map/ppermute | solution.py:416
  16.4 3.4 %copy-start = (f32[108,256]{1,0:T(8,128)}, f32[108,256]{1,0:T(8,128)S(1)}, u32[]{:S(2)}) copy-start(f32[108,256]{1,0:T(8,128)S(1)} %collective-permute-done.2.recv_c) | copy-start | bytes 331780
  19.8 0.6 %copy-start.1 = (f32[108,256]{1,0:T(8,128)}, f32[108,256]{1,0:T(8,128)S(1)}, u32[]{:S(2)}) copy-start(f32[108,256]{1,0:T(8,128)S(1)} %collective-permute-done.3.recv_d) | copy-start | bytes 331780
  23.2 14.8 %collective-permute-start.7 = (f32[10,8,256]{2,1,0:T(8,128)}, f32[10,8,256]{2,1,0:T(8,128)S(1)}, u32[]{:S(2)}, u32[]{:S(2)}) collective-permute-start(f32[10,8,256]{2,1,0:T(8,128)} %get-tuple-element.21), channel_id=1, source_target_pairs={{28,2},{29,0},{30,3},{31,1}} | collective-permute-start | bytes 245768 | tf_op jit(solution)/shard_map/ppermute | solution.py:438
  24.5 13.5 %collective-permute-start.6 = (f32[10,8,256]{2,1,0:T(8,128)}, f32[10,8,256]{2,1,0:T(8,128)S(1)}, u32[]{:S(2)}, u32[]{:S(2)}) collective-permute-start(f32[10,8,256]{2,1,0:T(8,128)} %get-tuple-element.21), channel_id=1, source_target_pairs={{28,0},{29,2},{30,1},{31,3}} | collective-permute-start | bytes 245768 | tf_op jit(solution)/shard_map/ppermute | solution.py:437
  25.8 4.0 %collective-permute-start.4 = (f32[2,8,256]{2,1,0:T(8,128)}, f32[2,8,256]{2,1,0:T(8,128)S(1)}, u32[]{:S(2)}, u32[]{:S(2)}) collective-permute-start(f32[2,8,256]{2,1,0:T(8,128)} %get-tuple-element.19), channel_id=1, source_target_pairs={{0,4},{4,0},{8,12},{12,8},{16,20},{20,16},{24,28},{28,24},{1,5},{5... | collective-permute-start | bytes 49160 | tf_op jit(solution)/shard_map/ppermute | solution.py:435
  29.8 8.3 %copy-start.6 = (f32[2,8,256]{2,1,0:T(8,128)}, f32[2,8,256]{2,1,0:T(8,128)S(1)}, u32[]{:S(2)}) copy-start(f32[2,8,256]{2,1,0:T(8,128)S(1)} %collective-permute-done.4.corner_a) | copy-start | bytes 49156
  29.8 8.2 %collective-permute-start.5 = (f32[2,8,256]{2,1,0:T(8,128)}, f32[2,8,256]{2,1,0:T(8,128)S(1)}, u32[]{:S(2)}, u32[]{:S(2)}) collective-permute-start(f32[2,8,256]{2,1,0:T(8,128)} %get-tuple-element.20), channel_id=1, source_target_pairs={{4,8},{8,4},{12,16},{16,12},{20,24},{24,20},{28,0},{0,28},{5,9},{9... | collective-permute-start | bytes 49160 | tf_op jit(solution)/shard_map/ppermute | solution.py:436
  38.0 0.6 %copy-start.7 = (f32[2,8,256]{2,1,0:T(8,128)}, f32[2,8,256]{2,1,0:T(8,128)S(1)}, u32[]{:S(2)}) copy-start(f32[2,8,256]{2,1,0:T(8,128)S(1)} %collective-permute-done.5.corner_b) | copy-start | bytes 49156
  38.0 0.6 %copy-start.4 = (f32[10,8,256]{2,1,0:T(8,128)}, f32[10,8,256]{2,1,0:T(8,128)S(1)}, u32[]{:S(2)}) copy-start(f32[10,8,256]{2,1,0:T(8,128)S(1)} %collective-permute-done.7.inlet_b) | copy-start | bytes 245764
  38.1 0.7 %copy-start.5 = (f32[10,8,256]{2,1,0:T(8,128)}, f32[10,8,256]{2,1,0:T(8,128)S(1)}, u32[]{:S(2)}) copy-start(f32[10,8,256]{2,1,0:T(8,128)S(1)} %collective-permute-done.6.inlet_a) | copy-start | bytes 245764
  38.1 0.7 %copy-start.2 = (f32[9,24,256]{2,1,0:T(8,128)}, f32[9,24,256]{2,1,0:T(8,128)S(1)}, u32[]{:S(2)}) copy-start(f32[9,24,256]{2,1,0:T(8,128)S(1)} %collective-permute-done.recv_a) | copy-start | bytes 663556
  38.1 0.8 %copy-start.3 = (f32[9,24,256]{2,1,0:T(8,128)}, f32[9,24,256]{2,1,0:T(8,128)S(1)}, u32[]{:S(2)}) copy-start(f32[9,24,256]{2,1,0:T(8,128)S(1)} %collective-permute-done.1.recv_b) | copy-start | bytes 663556
where the time goes:
time: 45.1 us; the launch traced here: 44.8 us
  starting transfers between devices  17.1 us (38%)
  Pallas kernels  16.2 us (36%)
  waiting for transfers between devices  9.28 us (21%)
  local copies, waits for them, and re-layouts  1.46 us (3%)
  between operations  0.73 us (2%)
    pallas_call x1, Pallas kernels, shards(): pl.pallas_call(collide_kernel, out_shape=(jax.ShapeDtypeStruct(main_pops....  7.53 us
    ppermute x1, starting transfers between devices, shards(): corner_b = lax.ppermute(corner_b, 'gx', swap_pairs(count_x, 1))  6.27 us
    pallas_call x1, Pallas kernels, shards(): pl.pallas_call(stream_kernel, out_shape=(jax.ShapeDtypeStruct(main_pops.s...  5.89 us
    ppermute x1, waiting for transfers between devices, shards(): corner_a = lax.ppermute(corner_a, 'gx', swap_pairs(count_x, 0))  3.94 us
    ppermute x1, starting transfers between devices, shards(): recv_b = lax.ppermute(send_b, 'gx', swap_pairs(count_x, 1))  3.54 us
    ppermute x1, waiting for transfers between devices, shards(): recv_d = lax.ppermute(send_d, 'gy', swap_pairs(count_y, 1))  3.4 us
    ppermute x1, starting transfers between devices, shards(): recv_a = lax.ppermute(send_a, 'gx', swap_pairs(count_x, 0))  3.03 us
    pallas_call x1, Pallas kernels, shards(): pl.pallas_call(corner_kernel, out_shape=(corner, corner, jax.ShapeDtypeSt...  2.82 us
  transfers between devices with their start and end apart: 8, of which 3 were waited for; matrix products, arithmetic and copies ran while one was open for 0% of the time, Pallas kernels for 6%

commit v1 on v0

v1 whole, which is shorter than its diff:
```python
import jax
import jax.numpy as jnp
import numpy as np
from jax import lax
from jax.experimental import pallas as pl
from jax.experimental.pallas import tpu as pltpu
from jax.sharding import PartitionSpec as P

drag_scale = -0.5 * 0.75
vmem_bytes = 20 * 1024 * 1024
any_space = pl.BlockSpec(memory_space=pltpu.HBM)
vmem_space = pl.BlockSpec(memory_space=pltpu.VMEM)
smem_space = pl.BlockSpec(memory_space=pltpu.SMEM)


def in_vmem(value):
    return pltpu.with_memory_space_constraint(value, pltpu.VMEM)


def in_hbm(value):
    return pltpu.with_memory_space_constraint(value, pltpu.HBM)


def swap_pairs(count, first):
    pairs = [(i, (i + 1) % count) for i in range(first, count, 2)]
    return [p for a, b in pairs for p in ((a, b), (b, a))]


def along_axes(values, stride, step):
    out = list(values)
    for start in range(27):
        if (start // stride) % 3 == 0:
            where = (start, start + stride, start + 2 * stride)
            for place, value in zip(where, step(*(values[i] for i in where))):
                out[place] = value
    return out


def to_moments(low, mid, high):
    outer = low + high
    return outer + mid, high - low, outer


def from_moments(zeroth, first, second):
    low, high = second - first, second + first
    return low, zeroth - (low + high), high


def digits(k):
    return k // 9, k // 3 % 3, k % 3


def moment_scales(rates_ref):
    keep, pull = [], []
    for k in range(27):
        ones = digits(k).count(1)
        twos = digits(k).count(2)
        half = 0.5 ** (ones + twos)
        third = 3.0 ** -(twos if ones else max(twos - 1, 0))
        rate = rates_ref[k]
        keep.append((1.0 - rate) * half)
        pull.append(rate * (half * third))
    return keep, pull


def relaxed_tile(pops, keep, pull, disk):
    m = pops
    for stride in (1, 3, 9):
        m = along_axes(m, stride, to_moments)
    density, flux = m[0], (m[9], m[3], m[1])
    inverse = 1.0 / density
    speed = [f * inverse for f in flux]
    third = density * (1.0 / 3.0)
    product = {(a, b): flux[a] * speed[b] for a in range(3) for b in range(a, 3)}
    drag = None
    if disk is not None:
        drag = jnp.where(disk, drag_scale * flux[0] * jnp.abs(speed[0]), 0.0)
    target = []
    for k in range(27):
        ones = [a for a in range(3) if digits(k)[a] == 1]
        twos = [a for a in range(3) if digits(k)[a] == 2]
        half = 0.5 ** (len(ones) + len(twos))
        if not ones and not twos:
            value = density
        elif len(ones) == 1 and not twos:
            value = m[k] * half
        elif len(ones) == 3:
            value = m[k] * keep[k]
        else:
            if len(ones) == 1:
                pulled = flux[ones[0]]
            elif len(ones) == 2:
                pulled = product[tuple(ones)]
            else:
                pulled = third
                for a in twos:
                    pulled = pulled + product[a, a]
            value = m[k] * keep[k] + pulled * pull[k]
        if drag is not None and ones == [0]:
            value = value + drag * (half * 3.0 ** -len(twos))
        target.append(value)
    for stride in (9, 3, 1):
        target = along_axes(target, stride, from_moments)
    return target


def collide_kernel(
    main_hbm, prec_hbm, cells_hbm, rates_ref,
    rel_main, rel_prec, send_a, send_b, send_c, send_d, inlet_send,
    main_in, prec_in, cells_in, in_sem, cell_sem,
):
    extent_x, extent_y, depth = main_in.shape[1:]
    prec_x, prec_y = prec_in.shape[1:3]
    odd_x = lax.rem(lax.axis_index("gx"), 2)
    odd_y = lax.rem(lax.axis_index("gy"), 2)

    def fetch_main(x):
        return pltpu.make_async_copy(main_hbm.at[:, x], main_in.at[:, x], in_sem.at[x])

    def fetch_prec(x):
        return pltpu.make_async_copy(
            prec_hbm.at[:, x], prec_in.at[:, x], in_sem.at[extent_x + x]
        )

    fetch_cells = pltpu.make_async_copy(cells_hbm, cells_in, cell_sem)
    for x in range(prec_x):
        fetch_prec(x).start()
    fetch_cells.start()
    for x in range(extent_x):
        fetch_main(x).start()
    keep, pull = moment_scales(rates_ref)

    def prec_plane(x, carry):
        fetch_prec(x).wait()
        for y in range(0, prec_y, 8):
            for z in range(0, depth, 128):
                rows, lanes = pl.ds(y, 8), pl.ds(z, 128)
                pops = [prec_in[i, x, rows, lanes] for i in range(27)]
                for i, value in enumerate(relaxed_tile(pops, keep, pull, None)):
                    rel_prec[i, x, rows, lanes] = value
        return carry

    def main_plane(x, carry):
        fetch_main(x).wait()
        for y in range(0, extent_y, 8):
            for z in range(0, depth, 128):
                rows, lanes = pl.ds(y, 8), pl.ds(z, 128)
                kind = cells_in[x, rows, lanes]
                pops = [main_in[i, x, rows, lanes] for i in range(27)]
                for i, value in enumerate(relaxed_tile(pops, keep, pull, kind == 2)):
                    if z == 0:
                        value = jnp.where(kind == 1, main_in[26 - i, x, rows, lanes], value)
                    rel_main[i, x, rows, lanes] = value
        return carry

    lax.fori_loop(0, prec_x, prec_plane, 0)
    fetch_cells.wait()
    lax.fori_loop(0, extent_x, main_plane, 0)

    def pick(odd, even_value, odd_value):
        return jnp.where(odd == 0, even_value, odd_value)

    planes = extent_x + prec_x
    for rel, first, size_x, size_y in (
        (rel_main, 0, extent_x, extent_y),
        (rel_prec, extent_y, prec_x, prec_y),
    ):
        for i in range(9):
            high, low = rel[18 + i, size_x - 1], rel[i, 0]
            send_a[i, first : first + size_y] = pick(odd_x, high, low)
            send_b[i, first : first + size_y] = pick(odd_x, low, high)
    inlet_send[...] = rel_prec[18:27, prec_x - 1]
    for pair in range(9):
        down, up = 9 * (pair // 3) + pair % 3, 9 * (pair // 3) + 6 + pair % 3
        for rel, first, size_x, size_y in (
            (rel_main, 0, extent_x, extent_y),
            (rel_prec, extent_x, prec_x, prec_y),
        ):
            for x in range(size_x):
                place = pl.ds(pair * planes + first + x, 1)
                low, high = rel[down, x, 0:1, :], rel[up, x, size_y - 1 : size_y, :]
                send_c[place, :] = pick(odd_y, high, low)
                send_d[place, :] = pick(odd_y, low, high)
    for step in range(3):
        place = pl.ds(9 * planes + step, 1)
        first, last = outlet_rows(rel_prec, step)
        send_c[place, :] = pick(odd_y, first, last)


def outlet_rows(rel_prec, step):
    prec_x, prec_y = rel_prec.shape[1:3]
    first = rel_prec[18 + step, prec_x - 1, 0:1, :]
    return first, rel_prec[24 + step, prec_x - 1, prec_y - 1 : prec_y, :]


def relay_kernel(send_d, recv_c, relayed_d):
    own = recv_c.shape[0] // 9 * 9
    relayed_d[0:own] = send_d[0:own]
    for step in range(recv_c.shape[0] - own):
        place = pl.ds(own + step, 1)
        relayed_d[place, :] = recv_c[place, :]


def own_rows_kernel(rel_prec, own_rows):
    own_rows[...] = jnp.zeros_like(own_rows)
    for step in range(3):
        first, last = outlet_rows(rel_prec, step)
        own_rows[step : step + 1, :] = last
        own_rows[3 + step : 4 + step, :] = first


def side_rows(recv_c, recv_d, odd_y, place):
    one, other = recv_c[pl.ds(place, 1), :], recv_d[pl.ds(place, 1), :]
    return jnp.where(odd_y == 0, other, one), jnp.where(odd_y == 0, one, other)


def corner_kernel(rel_prec, recv_c, recv_d, *rest):
    fetched, (corner_a, corner_b) = rest[:-2], rest[-2:]
    prec_x, prec_y = rel_prec.shape[1:3]
    planes = recv_c.shape[0] // 9
    extent_x = planes - prec_x
    place_x, place_y = lax.axis_index("gx"), lax.axis_index("gy")
    count_y = lax.axis_size("gy")
    odd_x, odd_y = lax.rem(place_x, 2), lax.rem(place_y, 2)
    at_last = place_x == lax.axis_size("gx") - 1

    def inlet_rows(step, low, high):
        if fetched:
            near = place_y < count_y // 2
            last = jnp.where(
                near, fetched[0][step : step + 1, :], fetched[1][step : step + 1, :]
            )
            first = jnp.where(
                near, fetched[2][3 + step : 4 + step, :], fetched[3][3 + step : 4 + step, :]
            )
            return last, first
        own_first, own_last = outlet_rows(rel_prec, step)
        beside = recv_c[pl.ds(9 * planes + step, 1), :]
        beyond = recv_d[pl.ds(9 * planes + step, 1), :]

        def choose(*options):
            value = options[0]
            for k in range(1, 4):
                value = jnp.where(place_y == k, options[k], value)
            return value

        return choose(low, own_last, beside, beyond), choose(beyond, beside, own_first, high)

    corner_a[...] = jnp.zeros_like(corner_a)
    corner_b[...] = jnp.zeros_like(corner_b)
    for step in range(3):
        outlet = side_rows(recv_c, recv_d, odd_y, (6 + step) * planes + planes - 1)
        inlet = inlet_rows(step, outlet[0], outlet[1])
        for lattice, (x_low, x_high) in enumerate(
            ((0, extent_x - 1), (extent_x, planes - 1))
        ):
            lows = side_rows(recv_c, recv_d, odd_y, step * planes + x_low)
            highs = side_rows(recv_c, recv_d, odd_y, (6 + step) * planes + x_high)
            for k in range(2):
                place = pl.ds(3 * k + step, 1)
                low, high = lows[k], highs[k]
                corner_a[lattice, place, :] = jnp.where(odd_x == 0, high, low)
                value = jnp.where(odd_x == 0, low, high)
                if lattice == 0:
                    value = jnp.where(at_last, inlet[k], value)
                corner_b[lattice, place, :] = value


def streamed(i, x, rel, source_rows, halo_row):
    size_y, depth = rel.shape[2:]
    _, step_y, step_z = (d - 1 for d in digits(i))
    value = source_rows
    if step_y:
        row = lax.broadcasted_iota(jnp.int32, (size_y, depth), 0)
        value = pltpu.roll(value, 1 if step_y == 1 else size_y - 1, 0)
        value = jnp.where(row == (0 if step_y == 1 else size_y - 1), halo_row, value)
    if step_z:
        lane = lax.broadcasted_iota(jnp.int32, (size_y, depth), 1)
        value = pltpu.roll(value, 1 if step_z == 1 else depth - 1, 1)
        value = jnp.where(lane == (0 if step_z == 1 else depth - 1), rel[26 - i, x], value)
    return value


def side_row(recv_c, recv_d, i, place, planes):
    step_x, step_y, step_z = (d - 1 for d in digits(i))
    odd = lax.rem(lax.axis_index("gy"), 2)
    where = pl.ds((3 * (step_x + 1) + step_z + 1) * planes + place, 1)
    from_low = odd if step_y == 1 else 1 - odd
    return jnp.where(from_low == 1, recv_c[where, :], recv_d[where, :])


def stream_kernel(
    rel_main, rel_prec, recv_c, recv_d, main_out, prec_out, main_v, prec_v, out_sem,
):
    planes = rel_main.shape[1] + rel_prec.shape[1]
    copies = []
    for rel, out_v, out_hbm, first in (
        (rel_main, main_v, main_out, 0),
        (rel_prec, prec_v, prec_out, rel_main.shape[1]),
    ):
        size_x = rel.shape[1]

        def emit(x, edges, rel=rel, out_v=out_v, first=first):
            for i in range(27):
                step_x, step_y, _ = (d - 1 for d in digits(i))
                if step_x in edges:
                    continue
                source = x - step_x
                halo = side_row(recv_c, recv_d, i, first + source, planes) if step_y else None
                out_v[i, x] = streamed(i, x, rel, rel[i, source], halo)

        def put(x, low, high, out_v=out_v, out_hbm=out_hbm, first=first):
            return pltpu.make_async_copy(
                out_v.at[low:high, x], out_hbm.at[low:high, x], out_sem.at[first + x]
            )

        def inner(x, carry, emit=emit, put=put):
            emit(x, ())
            put(x, 0, 27).start()
            return carry

        lax.fori_loop(1, size_x - 1, inner, 0)
        emit(0, (1,))
        copies.append(put(0, 0, 18))
        copies[-1].start()
        emit(size_x - 1, (-1,))
        copies.append(put(size_x - 1, 9, 27))
        copies[-1].start()
        copies.extend(put(x, 0, 27) for x in range(1, size_x - 1))
    for copy in copies:
        copy.wait()


def edge_kernel(
    rel_main, rel_prec, recv_a, recv_b, recv_c, recv_d, corner_a, corner_b, inlet_a, inlet_b,
    main_old, prec_old, main_out, prec_out, main_v, prec_v, out_sem,
):
    extent_x, extent_y, _ = rel_main.shape[1:]
    prec_x, prec_y = rel_prec.shape[1:3]
    planes = extent_x + prec_x
    place_x, place_y = lax.axis_index("gx"), lax.axis_index("gy")
    count_x, count_y = lax.axis_size("gx"), lax.axis_size("gy")
    odd_x = lax.rem(place_x, 2)
    at_first, at_last = place_x == 0, place_x == count_x - 1
    near = place_y < count_y // 2
    copies = []
    for rel, out_v, out_hbm, lattice in (
        (rel_prec, prec_v, prec_out, 1),
        (rel_main, main_v, main_out, 0),
    ):
        size_x, size_y = rel.shape[1:3]
        start_y = extent_y if lattice else 0
        for low_side in (True, False):
            x = 0 if low_side else size_x - 1
            from_one = odd_x if low_side else 1 - odd_x
            for part in range(9):
                i = part + (18 if low_side else 0)
                step_y, step_z = digits(i)[1] - 1, digits(i)[2] - 1
                rows = pl.ds(start_y, size_y)
                value = jnp.where(from_one == 1, recv_a[part, rows], recv_b[part, rows])
                halo = None
                if step_y:
                    where = pl.ds((0 if step_y == 1 else 3) + step_z + 1, 1)
                    halo = jnp.where(
                        from_one == 1, corner_a[lattice, where, :], corner_b[lattice, where, :]
                    )
                if not lattice and low_side:
                    lower = jnp.where(near, inlet_a[part], inlet_b[part])
                    upper = jnp.where(near, inlet_b[part], inlet_a[part])
                    whole = jnp.concatenate([lower, upper], axis=0)
                    value = jnp.where(at_first, whole, value)
                if not lattice and not low_side:
                    value = jnp.where(at_last, rel[i, size_x - 1], value)
                    if step_y:
                        row = side_row(recv_c, recv_d, i, size_x - 1, planes)
                        halo = jnp.where(at_last, row, halo)
                out_v[part, 0 if low_side else 1] = streamed(i, x, rel, value, halo)
            first = 18 if low_side else 0
            copy = pltpu.make_async_copy(
                out_v.at[:, 0 if low_side else 1],
                out_hbm.at[first : first + 9, x],
                out_sem.at[2 * lattice + (0 if low_side else 1)],
            )
            copy.start()
            copies.append(copy)
    for copy in copies:
        copy.wait()


def shards(prec_pops, main_pops, cell_type, rates):
    _, extent_x, extent_y, depth = main_pops.shape
    _, prec_x, prec_y, _ = prec_pops.shape
    count_x, count_y = lax.axis_size("gx"), lax.axis_size("gy")
    assert count_x % 2 == 0 and count_y % 2 == 0 and extent_y == 2 * prec_y
    planes = extent_x + prec_x
    f32 = jnp.float32
    face = (9, extent_y + prec_y, depth)
    side = (9 * planes + 3, depth)
    params = pltpu.CompilerParams(vmem_limit_bytes=vmem_bytes)
    dma = pltpu.SemaphoreType.DMA
    block = (9, prec_y, depth)
    main_rel, prec_rel, send_a, send_b, send_c, send_d, inlet_send = pl.pallas_call(
        collide_kernel,
        out_shape=tuple(
            pltpu.VMEM(shape, f32)
            for shape in (main_pops.shape, prec_pops.shape, face, face, side, side, block)
        ),
        in_specs=[any_space] * 3 + [smem_space],
        out_specs=(vmem_space,) * 7,
        scratch_shapes=[
            pltpu.VMEM(main_pops.shape, f32),
            pltpu.VMEM(prec_pops.shape, f32),
            pltpu.VMEM(cell_type.shape, jnp.int32),
            dma((planes,)), dma(()),
        ],
        compiler_params=params,
        name="collide",
    )(in_hbm(main_pops), in_hbm(prec_pops), in_hbm(cell_type), in_hbm(rates))
    main_rel, prec_rel = in_vmem(main_rel), in_vmem(prec_rel)

    half = count_y // 2
    base = (count_x - 1) * count_y
    near = [(base + s, s // 2 + half * (s % 2)) for s in range(count_y)]
    far = [(base + s, s // 2 + half * (1 - s % 2)) for s in range(count_y)]
    recv_a = in_vmem(lax.ppermute(send_a, "gx", swap_pairs(count_x, 0)))
    recv_b = in_vmem(lax.ppermute(send_b, "gx", swap_pairs(count_x, 1)))
    inlet_a = in_vmem(lax.ppermute(inlet_send, ("gx", "gy"), near))
    inlet_b = in_vmem(lax.ppermute(inlet_send, ("gx", "gy"), far))
    recv_c = in_vmem(lax.ppermute(send_c, "gy", swap_pairs(count_y, 0)))
    fetched = []
    if count_y == 4:
        send_d = pl.pallas_call(
            relay_kernel,
            out_shape=pltpu.VMEM(side, f32),
            in_specs=[vmem_space] * 2,
            out_specs=vmem_space,
            compiler_params=params,
            name="relay",
        )(in_vmem(send_d), recv_c)
    else:
        own_rows = pl.pallas_call(
            own_rows_kernel,
            out_shape=pltpu.VMEM((8, depth), f32),
            in_specs=[vmem_space],
            out_specs=vmem_space,
            compiler_params=params,
            name="outlet_rows",
        )(prec_rel)
        for shift in (-1, 2):
            for start in (0, half):
                pairs = [((2 * j + shift) % count_y, j) for j in range(start, start + half)]
                fetched.append(in_vmem(lax.ppermute(own_rows, "gy", pairs)))
    recv_d = in_vmem(lax.ppermute(send_d, "gy", swap_pairs(count_y, 1)))

    corner = (2, 8, depth)
    corner_a, corner_b = pl.pallas_call(
        corner_kernel,
        out_shape=(pltpu.VMEM(corner, f32),) * 2,
        in_specs=[vmem_space] * (3 + len(fetched)),
        out_specs=(vmem_space,) * 2,
        compiler_params=params,
        name="corners",
    )(prec_rel, recv_c, recv_d, *fetched)
    corner_a = in_vmem(lax.ppermute(corner_a, "gx", swap_pairs(count_x, 0)))
    corner_b = in_vmem(lax.ppermute(corner_b, "gx", swap_pairs(count_x, 1)))

    outs = (
        jax.ShapeDtypeStruct(main_pops.shape, f32),
        jax.ShapeDtypeStruct(prec_pops.shape, f32),
    )
    main_part, prec_part = pl.pallas_call(
        stream_kernel,
        out_shape=outs,
        in_specs=[vmem_space] * 4,
        out_specs=(any_space, any_space),
        scratch_shapes=[
            pltpu.VMEM(main_pops.shape, f32),
            pltpu.VMEM(prec_pops.shape, f32),
            dma((planes,)),
        ],
        compiler_params=params,
        name="stream",
    )(main_rel, prec_rel, recv_c, recv_d)
    main_next, prec_next = pl.pallas_call(
        edge_kernel,
        out_shape=outs,
        in_specs=[vmem_space] * 10 + [any_space] * 2,
        out_specs=(any_space, any_space),
        scratch_shapes=[
            pltpu.VMEM((9, 2, extent_y, depth), f32),
            pltpu.VMEM((9, 2, prec_y, depth), f32),
            dma((4,)),
        ],
        input_output_aliases={10: 0, 11: 1},
        compiler_params=params,
        name="edges",
    )(
        main_rel, prec_rel, recv_a, recv_b, recv_c, recv_d,
        corner_a, corner_b, inlet_a, inlet_b, main_part, prec_part,
    )
    return prec_next, main_next


def solution(mesh):
    placed = (P(None, "gx", "gy", None), P(None, "gx", "gy", None), P("gx", "gy", None), P())
    return jax.shard_map(
        shards,
        mesh=mesh,
        in_specs=placed,
        out_specs=(P(None, "gx", "gy", None), P(None, "gx", "gy", None)),
        check_vma=False,
    )
```

time: 45.1 us -> 29.3 us (0.65)
  Pallas kernels: 16.2 us -> 7.94 us
  starting transfers between devices: 17.1 us -> 10.7 us
  local copies, waits for them, and re-layouts: 1.46 us -> 0 us
  waiting for transfers between devices: 9.28 us -> 9.79 us
    pallas_call x3 -> x5, Pallas kernels: 16.2 us -> 7.94 us  [the longest x1 4.78 us: shards(): pl.pallas_call(collide_kernel, out_shape=tuple((pltpu.VMEM(shape, f32) fo...]
    ppermute x8, starting transfers between devices: 17.1 us -> 10.7 us  [the longest x1 3.54 us: shards(): recv_b = in_vmem(lax.ppermute(send_b, 'gx', swap_pairs(count_x, 1)))]
    unnamed x16 -> x0, local copies, waits for them, and re-layouts: 1.46 us -> none
    ppermute x8, waiting for transfers between devices: 9.28 us -> 9.79 us  [the longest x1 4.15 us: shards(): inlet_b = in_vmem(lax.ppermute(inlet_send, ('gx', 'gy'), far))]
  transfers between devices with their start and end apart: 8 -> 8, of which waited for: 3 -> 3; matrix products, arithmetic and copies ran while one was open for 0% -> 0% of each run, Pallas kernels for 6% -> 8%
where the time goes in v1:
time: 29.3 us; the launch traced here: 29.1 us
  starting transfers between devices  10.7 us (37%)
  waiting for transfers between devices  9.79 us (33%)
  Pallas kernels  7.94 us (27%)
  between operations  0.72 us (2%)
    pallas_call x1, Pallas kernels, shards(): pl.pallas_call(collide_kernel, out_shape=tuple((pltpu.VMEM(shape, f32) fo...  4.78 us
    ppermute x1, waiting for transfers between devices, shards(): inlet_b = in_vmem(lax.ppermute(inlet_send, ('gx', 'gy'), far))  4.15 us
    ppermute x1, waiting for transfers between devices, shards(): corner_b = in_vmem(lax.ppermute(corner_b, 'gx', swap_pairs(count_x, 1)))  3.82 us
    ppermute x1, starting transfers between devices, shards(): recv_b = in_vmem(lax.ppermute(send_b, 'gx', swap_pairs(count_x, 1)))  3.54 us
    ppermute x1, starting transfers between devices, shards(): recv_a = in_vmem(lax.ppermute(send_a, 'gx', swap_pairs(count_x, 0)))  2.59 us
    pallas_call x1, Pallas kernels, shards(): pl.pallas_call(stream_kernel, out_shape=outs, in_specs=[vmem_space] * 4,...  2.23 us
    ppermute x1, waiting for transfers between devices, shards(): recv_d = in_vmem(lax.ppermute(send_d, 'gy', swap_pairs(count_y, 1)))  1.81 us
    ppermute x1, starting transfers between devices, shards(): inlet_a = in_vmem(lax.ppermute(inlet_send, ('gx', 'gy'), near))  1.29 us
  transfers between devices with their start and end apart: 8, of which 3 were waited for; matrix products, arithmetic and copies ran while one was open for 0% of the time, Pallas kernels for 8%

profile of v1, /device:TPU:0, one launch (start us, length us, event | category | flops | bytes accessed | tf_op | source)
XLA Modules:
  0.0 29.1 jit_solution(3425819029258985295)
XLA Ops:
  0.6 4.8 %collide.1 = (f32[27,8,16,256]{3,2,1,0:T(8,128)S(1)}, f32[27,4,8,256]{3,2,1,0:T(8,128)S(1)}, f32[9,24,256]{2,1,0:T(8,128)S(1)}, f32[9,24,256]{2,1,0:T(8,128)S(1)...) custom-call(f32[27,8,16,256]{3,2,1,0:T(8,128)} %main_hbm.1, ...), custom_call_target="tpu_custom_call" | custom-call | tf_op jit(solution)/shard_map/collide/pallas_call | solution.py:402
  5.4 0.5 %collective-permute-start.2 = (f32[111,256]{1,0:T(8,128)S(1)}, f32[111,256]{1,0:T(8,128)S(1)}, u32[]{:S(2)}, u32[]{:S(2)}) collective-permute-start(f32[111,256]{1,0:T(8,128)S(1)} %get-tuple-element.19), channel_id=1, source_target_pairs={{0,1},{1,0},{2,3},{3,2},{4,5},{5,4},{6,7},{7,6},{8,9},{9,8},{10,11... | collective-permute-start | bytes 341000 | tf_op jit(solution)/shard_map/ppermute | solution.py:429
  5.9 2.6 %collective-permute-start = (f32[9,24,256]{2,1,0:T(8,128)S(1)}, f32[9,24,256]{2,1,0:T(8,128)S(1)}, u32[]{:S(2)}, u32[]{:S(2)}) collective-permute-start(f32[9,24,256]{2,1,0:T(8,128)S(1)} %get-tuple-element.17), channel_id=1, source_target_pairs={{0,4},{4,0},{8,12},{12,8},{16,20},{20,16},{24,28},{28,24},{1,5},{5... | collective-permute-start | bytes 663560 | tf_op jit(solution)/shard_map/ppermute | solution.py:425
  8.5 3.5 %collective-permute-start.1 = (f32[9,24,256]{2,1,0:T(8,128)S(1)}, f32[9,24,256]{2,1,0:T(8,128)S(1)}, u32[]{:S(2)}, u32[]{:S(2)}) collective-permute-start(f32[9,24,256]{2,1,0:T(8,128)S(1)} %get-tuple-element.18), channel_id=1, source_target_pairs={{4,8},{8,4},{12,16},{16,12},{20,24},{24,20},{28,0},{0,28},{5,9},{9... | collective-permute-start | bytes 663560 | tf_op jit(solution)/shard_map/ppermute | solution.py:426
  12.1 0.0 collective-permute-done.2.recv_c
  12.1 1.0 %collective-permute-start.3 = (f32[111,256]{1,0:T(8,128)S(1)}, f32[111,256]{1,0:T(8,128)S(1)}, u32[]{:S(2)}, u32[]{:S(2)}) collective-permute-start(f32[111,256]{1,0:T(8,128)S(1)} %relay.1), channel_id=1, source_target_pairs={{1,2},{2,1},{3,0},{0,3},{5,6},{6,5},{7,4},{4,7},{9,10},{10,9},{11,... | collective-permute-start | bytes 341000 | tf_op jit(solution)/shard_map/ppermute | solution.py:453
  13.1 1.3 %collective-permute-start.7 = (f32[9,8,256]{2,1,0:T(8,128)S(1)}, f32[9,8,256]{2,1,0:T(8,128)S(1)}, u32[]{:S(2)}, u32[]{:S(2)}) collective-permute-start(f32[9,8,256]{2,1,0:T(8,128)S(1)} %get-tuple-element.23), channel_id=1, source_target_pairs={{28,2},{29,0},{30,3},{31,1}} | collective-permute-start | bytes 221192 | tf_op jit(solution)/shard_map/ppermute | solution.py:428
  14.4 1.3 %collective-permute-start.6 = (f32[9,8,256]{2,1,0:T(8,128)S(1)}, f32[9,8,256]{2,1,0:T(8,128)S(1)}, u32[]{:S(2)}, u32[]{:S(2)}) collective-permute-start(f32[9,8,256]{2,1,0:T(8,128)S(1)} %get-tuple-element.23), channel_id=1, source_target_pairs={{28,0},{29,2},{30,1},{31,3}} | collective-permute-start | bytes 221192 | tf_op jit(solution)/shard_map/ppermute | solution.py:427
  15.7 1.8 %collective-permute-done.3.recv_d = f32[111,256]{1,0:T(8,128)S(1)} collective-permute-done((f32[111,256]{1,0:T(8,128)S(1)}, f32[111,256]{1,0:T(8,128)S(1)}, u32[]{:S(2)}, u32[]{:S(2)}) %collective-permute-start.3) | collective-permute-done | bytes 113696 | tf_op jit(solution)/shard_map/ppermute | solution.py:453
  17.6 0.1 collective-permute-start.4
  17.7 4.2 %collective-permute-done.7.inlet_b = f32[9,8,256]{2,1,0:T(8,128)S(1)} collective-permute-done((f32[9,8,256]{2,1,0:T(8,128)S(1)}, f32[9,8,256]{2,1,0:T(8,128)S(1)}, u32[]{:S(2)}, u32[]{:S(2)}) %collective-permute-start.7) | collective-permute-done | bytes 73760 | tf_op jit(solution)/shard_map/ppermute | solution.py:428
  21.8 0.3 %collective-permute-start.5 = (f32[2,8,256]{2,1,0:T(8,128)S(1)}, f32[2,8,256]{2,1,0:T(8,128)S(1)}, u32[]{:S(2)}, u32[]{:S(2)}) collective-permute-start(f32[2,8,256]{2,1,0:T(8,128)S(1)} %get-tuple-element.22), channel_id=1, source_target_pairs={{4,8},{8,4},{12,16},{16,12},{20,24},{24,20},{28,0},{0,28},{5,9},{9... | collective-permute-start | bytes 49160 | tf_op jit(solution)/shard_map/ppermute | solution.py:465
  22.1 2.2 %stream.1 = (f32[27,8,16,256]{3,2,1,0:T(8,128)}, f32[27,4,8,256]{3,2,1,0:T(8,128)}) custom-call(f32[27,8,16,256]{3,2,1,0:T(8,128)S(1)} %get-tuple-element.15.rel_main, f32[27,4,8,256]{3,2,1,0:T(8,128)S(1)} %get-tuple-element.16.rel_prec, f32[111,256]{1,0:T(8,128)S(1)} %collective-permute-done.2.recv_c, f32[111,256]{1,0:T(8,128)S(1)} %collective-permute-done.3.recv_d), custom_call_target="tpu_custom_call" | custom-call | tf_op jit(solution)/shard_map/stream/pallas_call | solution.py:471
  24.4 0.0 collective-permute-done.6.inlet_a
  24.4 0.0 collective-permute-done.recv_a
  24.4 0.0 collective-permute-done.1.recv_b
  24.4 0.0 collective-permute-done.4.corner_a
  24.4 3.8 %collective-permute-done.5.corner_b = f32[2,8,256]{2,1,0:T(8,128)S(1)} collective-permute-done((f32[2,8,256]{2,1,0:T(8,128)S(1)}, f32[2,8,256]{2,1,0:T(8,128)S(1)}, u32[]{:S(2)}, u32[]{:S(2)}) %collective-permute-start.5) | collective-permute-done | bytes 16416 | tf_op jit(solution)/shard_map/ppermute | solution.py:465
  28.2 0.9 %edges.1 = (f32[27,8,16,256]{3,2,1,0:T(8,128)}, f32[27,4,8,256]{3,2,1,0:T(8,128)}) custom-call(f32[27,8,16,256]{3,2,1,0:T(8,128)S(1)} %get-tuple-element.15.rel_main, f32[27,4,8,256]{3,2,1,0:T(8,128)S(1)} %get-tuple-element.16.rel_prec, f32[9,24,256]{2,1,0:T(8,128)S(1)} %collective-permute-done.recv_a, ...), custom_call_target="tpu_custom_call", output_to_operand_aliasing={{0}: (10, {}), {1}: (11, {})} | custom-call | tf_op jit(solution)/shard_map/edges/pallas_call | solution.py:484
  (2 shorter events, 0.0 us)
Async XLA Ops:
  5.4 6.7 %collective-permute-start.2 = (f32[111,256]{1,0:T(8,128)S(1)}, f32[111,256]{1,0:T(8,128)S(1)}, u32[]{:S(2)}, u32[]{:S(2)}) collective-permute-start(f32[111,256]{1,0:T(8,128)S(1)} %get-tuple-element.19), channel_id=1, source_target_pairs={{0,1},{1,0},{2,3},{3,2},{4,5},{5,4},{6,7},{7,6},{8,9},{9,8},{10,11... | collective-permute-start | bytes 341000 | tf_op jit(solution)/shard_map/ppermute | solution.py:429
  5.9 18.5 %collective-permute-start = (f32[9,24,256]{2,1,0:T(8,128)S(1)}, f32[9,24,256]{2,1,0:T(8,128)S(1)}, u32[]{:S(2)}, u32[]{:S(2)}) collective-permute-start(f32[9,24,256]{2,1,0:T(8,128)S(1)} %get-tuple-element.17), channel_id=1, source_target_pairs={{0,4},{4,0},{8,12},{12,8},{16,20},{20,16},{24,28},{28,24},{1,5},{5... | collective-permute-start | bytes 663560 | tf_op jit(solution)/shard_map/ppermute | solution.py:425
  8.5 15.9 %collective-permute-start.1 = (f32[9,24,256]{2,1,0:T(8,128)S(1)}, f32[9,24,256]{2,1,0:T(8,128)S(1)}, u32[]{:S(2)}, u32[]{:S(2)}) collective-permute-start(f32[9,24,256]{2,1,0:T(8,128)S(1)} %get-tuple-element.18), channel_id=1, source_target_pairs={{4,8},{8,4},{12,16},{16,12},{20,24},{24,20},{28,0},{0,28},{5,9},{9... | collective-permute-start | bytes 663560 | tf_op jit(solution)/shard_map/ppermute | solution.py:426
  12.1 5.4 %collective-permute-start.3 = (f32[111,256]{1,0:T(8,128)S(1)}, f32[111,256]{1,0:T(8,128)S(1)}, u32[]{:S(2)}, u32[]{:S(2)}) collective-permute-start(f32[111,256]{1,0:T(8,128)S(1)} %relay.1), channel_id=1, source_target_pairs={{1,2},{2,1},{3,0},{0,3},{5,6},{6,5},{7,4},{4,7},{9,10},{10,9},{11,... | collective-permute-start | bytes 341000 | tf_op jit(solution)/shard_map/ppermute | solution.py:453
  13.1 8.7 %collective-permute-start.7 = (f32[9,8,256]{2,1,0:T(8,128)S(1)}, f32[9,8,256]{2,1,0:T(8,128)S(1)}, u32[]{:S(2)}, u32[]{:S(2)}) collective-permute-start(f32[9,8,256]{2,1,0:T(8,128)S(1)} %get-tuple-element.23), channel_id=1, source_target_pairs={{28,2},{29,0},{30,3},{31,1}} | collective-permute-start | bytes 221192 | tf_op jit(solution)/shard_map/ppermute | solution.py:428
  14.4 10.0 %collective-permute-start.6 = (f32[9,8,256]{2,1,0:T(8,128)S(1)}, f32[9,8,256]{2,1,0:T(8,128)S(1)}, u32[]{:S(2)}, u32[]{:S(2)}) collective-permute-start(f32[9,8,256]{2,1,0:T(8,128)S(1)} %get-tuple-element.23), channel_id=1, source_target_pairs={{28,0},{29,2},{30,1},{31,3}} | collective-permute-start | bytes 221192 | tf_op jit(solution)/shard_map/ppermute | solution.py:427
  17.6 6.8 %collective-permute-start.4 = (f32[2,8,256]{2,1,0:T(8,128)S(1)}, f32[2,8,256]{2,1,0:T(8,128)S(1)}, u32[]{:S(2)}, u32[]{:S(2)}) collective-permute-start(f32[2,8,256]{2,1,0:T(8,128)S(1)} %get-tuple-element.21), channel_id=1, source_target_pairs={{0,4},{4,0},{8,12},{12,8},{16,20},{20,16},{24,28},{28,24},{1,5},{5... | collective-permute-start | bytes 49160 | tf_op jit(solution)/shard_map/ppermute | solution.py:464
  21.8 6.4 %collective-permute-start.5 = (f32[2,8,256]{2,1,0:T(8,128)S(1)}, f32[2,8,256]{2,1,0:T(8,128)S(1)}, u32[]{:S(2)}, u32[]{:S(2)}) collective-permute-start(f32[2,8,256]{2,1,0:T(8,128)S(1)} %get-tuple-element.22), channel_id=1, source_target_pairs={{4,8},{8,4},{12,16},{16,12},{20,24},{24,20},{28,0},{0,28},{5,9},{9... | collective-permute-start | bytes 49160 | tf_op jit(solution)/shard_map/ppermute | solution.py:465

commit v2 on v1

--- a/solution.py
+++ b/solution.py
@@ -168,7 +168,8 @@
         for i in range(9):
             high, low = rel[18 + i, size_x - 1], rel[i, 0]
             send_a[i, first : first + size_y] = pick(odd_x, high, low)
-            send_b[i, first : first + size_y] = pick(odd_x, low, high)
+            if first == 0:
+                send_b[i] = pick(odd_x, low, high)
     inlet_send[...] = rel_prec[18:27, prec_x - 1]
     for pair in range(9):
         down, up = 9 * (pair // 3) + pair % 3, 9 * (pair // 3) + 6 + pair % 3
@@ -214,7 +215,7 @@
     return jnp.where(odd_y == 0, other, one), jnp.where(odd_y == 0, one, other)
 
 
-def corner_kernel(rel_prec, recv_c, recv_d, *rest):
+def corner_kernel(rel_prec, recv_a, recv_c, recv_d, *rest):
     fetched, (corner_a, corner_b) = rest[:-2], rest[-2:]
     prec_x, prec_y = rel_prec.shape[1:3]
     planes = recv_c.shape[0] // 9
@@ -247,7 +248,9 @@
         return choose(low, own_last, beside, beyond), choose(beyond, beside, own_first, high)
 
     corner_a[...] = jnp.zeros_like(corner_a)
-    corner_b[...] = jnp.zeros_like(corner_b)
+    for i in range(9):
+        corner_b[i] = jnp.where(odd_x == 0, rel_prec[i, 0], rel_prec[18 + i, prec_x - 1])
+    corner_b[9:11] = jnp.zeros((2,) + corner_b.shape[1:], jnp.float32)
     for step in range(3):
         outlet = side_rows(recv_c, recv_d, odd_y, (6 + step) * planes + planes - 1)
         inlet = inlet_rows(step, outlet[0], outlet[1])
@@ -263,7 +266,7 @@
                 value = jnp.where(odd_x == 0, low, high)
                 if lattice == 0:
                     value = jnp.where(at_last, inlet[k], value)
-                corner_b[lattice, place, :] = value
+                corner_b[9 + lattice, place, :] = value
 
 
 def streamed(i, x, rel, source_rows, halo_row):
@@ -290,7 +293,8 @@
 
 
 def stream_kernel(
-    rel_main, rel_prec, recv_c, recv_d, main_out, prec_out, main_v, prec_v, out_sem,
+    rel_main, rel_prec, recv_c, recv_d, inlet_a, inlet_b,
+    main_out, prec_out, main_v, prec_v, out_sem,
 ):
     planes = rel_main.shape[1] + rel_prec.shape[1]
     copies = []
@@ -357,12 +361,13 @@
                 i = part + (18 if low_side else 0)
                 step_y, step_z = digits(i)[1] - 1, digits(i)[2] - 1
                 rows = pl.ds(start_y, size_y)
-                value = jnp.where(from_one == 1, recv_a[part, rows], recv_b[part, rows])
+                other = corner_b[part] if lattice else recv_b[part]
+                value = jnp.where(from_one == 1, recv_a[part, rows], other)
                 halo = None
                 if step_y:
                     where = pl.ds((0 if step_y == 1 else 3) + step_z + 1, 1)
                     halo = jnp.where(
-                        from_one == 1, corner_a[lattice, where, :], corner_b[lattice, where, :]
+                        from_one == 1, corner_a[lattice, where, :], corner_b[9 + lattice, where, :]
                     )
                 if not lattice and low_side:
                     lower = jnp.where(near, inlet_a[part], inlet_b[part])
@@ -403,7 +408,9 @@
         collide_kernel,
         out_shape=tuple(
             pltpu.VMEM(shape, f32)
-            for shape in (main_pops.shape, prec_pops.shape, face, face, side, side, block)
+            for shape in (
+                main_pops.shape, prec_pops.shape, face, (9, extent_y, depth), side, side, block
+            )
         ),
         in_specs=[any_space] * 3 + [smem_space],
         out_specs=(vmem_space,) * 7,
@@ -423,7 +430,8 @@
     near = [(base + s, s // 2 + half * (s % 2)) for s in range(count_y)]
     far = [(base + s, s // 2 + half * (1 - s % 2)) for s in range(count_y)]
     recv_a = in_vmem(lax.ppermute(send_a, "gx", swap_pairs(count_x, 0)))
-    recv_b = in_vmem(lax.ppermute(send_b, "gx", swap_pairs(count_x, 1)))
+    across = [p for p in swap_pairs(count_x, 1) if abs(p[0] - p[1]) == 1]
+    recv_b = in_vmem(lax.ppermute(send_b, "gx", across))
     inlet_a = in_vmem(lax.ppermute(inlet_send, ("gx", "gy"), near))
     inlet_b = in_vmem(lax.ppermute(inlet_send, ("gx", "gy"), far))
     recv_c = in_vmem(lax.ppermute(send_c, "gy", swap_pairs(count_y, 0)))
@@ -455,12 +463,12 @@
     corner = (2, 8, depth)
     corner_a, corner_b = pl.pallas_call(
         corner_kernel,
-        out_shape=(pltpu.VMEM(corner, f32),) * 2,
-        in_specs=[vmem_space] * (3 + len(fetched)),
+        out_shape=(pltpu.VMEM(corner, f32), pltpu.VMEM((11, prec_y, depth), f32)),
+        in_specs=[vmem_space] * (4 + len(fetched)),
         out_specs=(vmem_space,) * 2,
         compiler_params=params,
         name="corners",
-    )(prec_rel, recv_c, recv_d, *fetched)
+    )(prec_rel, recv_a, recv_c, recv_d, *fetched)
     corner_a = in_vmem(lax.ppermute(corner_a, "gx", swap_pairs(count_x, 0)))
     corner_b = in_vmem(lax.ppermute(corner_b, "gx", swap_pairs(count_x, 1)))
 
@@ -471,7 +479,7 @@
     main_part, prec_part = pl.pallas_call(
         stream_kernel,
         out_shape=outs,
-        in_specs=[vmem_space] * 4,
+        in_specs=[vmem_space] * 6,
         out_specs=(any_space, any_space),
         scratch_shapes=[
             pltpu.VMEM(main_pops.shape, f32),
@@ -480,7 +488,8 @@
         ],
         compiler_params=params,
         name="stream",
-    )(main_rel, prec_rel, recv_c, recv_d)
+        cost_estimate=pl.CostEstimate(flops=10**9, bytes_accessed=1, transcendentals=0),
+    )(main_rel, prec_rel, recv_c, recv_d, inlet_a, inlet_b)
     main_next, prec_next = pl.pallas_call(
         edge_kernel,
         out_shape=outs,

time: 29.3 us -> 24.7 us (0.84)
  waiting for transfers between devices: 9.79 us -> 2.84 us
  starting transfers between devices: 10.7 us -> 13 us
    ppermute x1, waiting for transfers between devices: 4.15 us -> 0.01 us  [shards(): inlet_b = in_vmem(lax.ppermute(inlet_send, ('gx', 'gy'), far))]
    ppermute x1, waiting for transfers between devices: 3.82 us -> 0.59 us  [shards(): corner_b = in_vmem(lax.ppermute(corner_b, 'gx', swap_pairs(count_x, 1)))]
    ppermute x1, starting transfers between devices: 0.34 us -> 3.54 us  [shards(): corner_b = in_vmem(lax.ppermute(corner_b, 'gx', swap_pairs(count_x, 1)))]
    ppermute x1, starting transfers between devices: 3.54 us -> 0.67 us  [shards(): recv_b = in_vmem(lax.ppermute(send_b, 'gx', across))]
    ppermute x1, waiting for transfers between devices: 1.81 us -> 0.01 us  [shards(): recv_d = in_vmem(lax.ppermute(send_d, 'gy', swap_pairs(count_y, 1)))]
    ppermute x1, starting transfers between devices: 0.07 us -> 1.82 us  [shards(): corner_a = in_vmem(lax.ppermute(corner_a, 'gx', swap_pairs(count_x, 0)))]
    ppermute x1, waiting for transfers between devices: 0.01 us -> 1.41 us  [shards(): recv_a = in_vmem(lax.ppermute(send_a, 'gx', swap_pairs(count_x, 0)))]
    ppermute x1, waiting for transfers between devices: 0.01 us -> 0.83 us  [shards(): inlet_a = in_vmem(lax.ppermute(inlet_send, ('gx', 'gy'), near))]
  transfers between devices with their start and end apart: 8 -> 8, of which waited for: 3 -> 3; matrix products, arithmetic and copies ran while one was open for 0% -> 0% of each run, Pallas kernels for 8% -> 9%
where the time goes in v2:
time: 24.7 us; the launch traced here: 24.5 us
  starting transfers between devices  13 us (53%)
  Pallas kernels  7.95 us (32%)
  waiting for transfers between devices  2.84 us (11%)
  between operations  0.7 us (3%)
    pallas_call x1, Pallas kernels, shards(): pl.pallas_call(collide_kernel, out_shape=tuple((pltpu.VMEM(shape, f32) fo...  4.78 us
    ppermute x1, starting transfers between devices, shards(): corner_b = in_vmem(lax.ppermute(corner_b, 'gx', swap_pairs(count_x, 1)))  3.54 us
    ppermute x1, starting transfers between devices, shards(): recv_a = in_vmem(lax.ppermute(send_a, 'gx', swap_pairs(count_x, 0)))  2.59 us
    pallas_call x1, Pallas kernels, shards(): pl.pallas_call(stream_kernel, out_shape=outs, in_specs=[vmem_space] * 6,...  2.23 us
    ppermute x1, starting transfers between devices, shards(): corner_a = in_vmem(lax.ppermute(corner_a, 'gx', swap_pairs(count_x, 0)))  1.82 us
    ppermute x1, waiting for transfers between devices, shards(): recv_a = in_vmem(lax.ppermute(send_a, 'gx', swap_pairs(count_x, 0)))  1.41 us
    ppermute x1, starting transfers between devices, shards(): recv_d = in_vmem(lax.ppermute(send_d, 'gy', swap_pairs(count_y, 1)))  1.33 us
    ppermute x1, starting transfers between devices, shards(): inlet_a = in_vmem(lax.ppermute(inlet_send, ('gx', 'gy'), near))  1.29 us
  transfers between devices with their start and end apart: 8, of which 3 were waited for; matrix products, arithmetic and copies ran while one was open for 0% of the time, Pallas kernels for 9%

profile of v2, /device:TPU:0, one launch (start us, length us, event | category | flops | bytes accessed | tf_op | source)
XLA Modules:
  0.0 24.5 jit_solution(3086449325744331358)
XLA Ops:
  0.6 4.8 %collide.1 = (f32[27,8,16,256]{3,2,1,0:T(8,128)S(1)}, f32[27,4,8,256]{3,2,1,0:T(8,128)S(1)}, f32[9,24,256]{2,1,0:T(8,128)S(1)}, f32[9,16,256]{2,1,0:T(8,128)S(1)...) custom-call(f32[27,8,16,256]{3,2,1,0:T(8,128)} %main_hbm.1, ...), custom_call_target="tpu_custom_call" | custom-call | tf_op jit(solution)/shard_map/collide/pallas_call | solution.py:407
  5.4 0.5 %collective-permute-start.2 = (f32[111,256]{1,0:T(8,128)S(1)}, f32[111,256]{1,0:T(8,128)S(1)}, u32[]{:S(2)}, u32[]{:S(2)}) collective-permute-start(f32[111,256]{1,0:T(8,128)S(1)} %get-tuple-element.19), channel_id=1, source_target_pairs={{0,1},{1,0},{2,3},{3,2},{4,5},{5,4},{6,7},{7,6},{8,9},{9,8},{10,11... | collective-permute-start | bytes 341000 | tf_op jit(solution)/shard_map/ppermute | solution.py:437
  5.9 2.6 %collective-permute-start = (f32[9,24,256]{2,1,0:T(8,128)S(1)}, f32[9,24,256]{2,1,0:T(8,128)S(1)}, u32[]{:S(2)}, u32[]{:S(2)}) collective-permute-start(f32[9,24,256]{2,1,0:T(8,128)S(1)} %get-tuple-element.17), channel_id=1, source_target_pairs={{0,4},{4,0},{8,12},{12,8},{16,20},{20,16},{24,28},{28,24},{1,5},{5... | collective-permute-start | bytes 663560 | tf_op jit(solution)/shard_map/ppermute | solution.py:432
  8.5 0.0 collective-permute-done.2.recv_c
  8.5 1.3 %collective-permute-start.3 = (f32[111,256]{1,0:T(8,128)S(1)}, f32[111,256]{1,0:T(8,128)S(1)}, u32[]{:S(2)}, u32[]{:S(2)}) collective-permute-start(f32[111,256]{1,0:T(8,128)S(1)} %relay.1), channel_id=1, source_target_pairs={{1,2},{2,1},{3,0},{0,3},{5,6},{6,5},{7,4},{4,7},{9,10},{10,9},{11,... | collective-permute-start | bytes 341000 | tf_op jit(solution)/shard_map/ppermute | solution.py:461
  9.9 1.3 %collective-permute-start.7 = (f32[9,8,256]{2,1,0:T(8,128)S(1)}, f32[9,8,256]{2,1,0:T(8,128)S(1)}, u32[]{:S(2)}, u32[]{:S(2)}) collective-permute-start(f32[9,8,256]{2,1,0:T(8,128)S(1)} %get-tuple-element.23), channel_id=1, source_target_pairs={{28,2},{29,0},{30,3},{31,1}} | collective-permute-start | bytes 221192 | tf_op jit(solution)/shard_map/ppermute | solution.py:436
  11.2 1.3 %collective-permute-start.6 = (f32[9,8,256]{2,1,0:T(8,128)S(1)}, f32[9,8,256]{2,1,0:T(8,128)S(1)}, u32[]{:S(2)}, u32[]{:S(2)}) collective-permute-start(f32[9,8,256]{2,1,0:T(8,128)S(1)} %get-tuple-element.23), channel_id=1, source_target_pairs={{28,0},{29,2},{30,1},{31,3}} | collective-permute-start | bytes 221192 | tf_op jit(solution)/shard_map/ppermute | solution.py:435
  12.5 0.7 %collective-permute-start.1 = (f32[9,16,256]{2,1,0:T(8,128)S(1)}, f32[9,16,256]{2,1,0:T(8,128)S(1)}, u32[]{:S(2)}, u32[]{:S(2)}) collective-permute-start(f32[9,16,256]{2,1,0:T(8,128)S(1)} %get-tuple-element.18), channel_id=1, source_target_pairs={{4,8},{8,4},{12,16},{16,12},{20,24},{24,20},{5,9},{9,5},{13,17},{1... | collective-permute-start | bytes 442376 | tf_op jit(solution)/shard_map/ppermute | solution.py:434
  13.1 1.4 %collective-permute-done.recv_a = f32[9,24,256]{2,1,0:T(8,128)S(1)} collective-permute-done((f32[9,24,256]{2,1,0:T(8,128)S(1)}, f32[9,24,256]{2,1,0:T(8,128)S(1)}, u32[]{:S(2)}, u32[]{:S(2)}) %collective-permute-start) | collective-permute-done | bytes 221216 | tf_op jit(solution)/shard_map/ppermute | solution.py:432
  14.6 0.0 collective-permute-done.3.recv_d
  14.6 1.8 %collective-permute-start.4 = (f32[2,8,256]{2,1,0:T(8,128)S(1)}, f32[2,8,256]{2,1,0:T(8,128)S(1)}, u32[]{:S(2)}, u32[]{:S(2)}) collective-permute-start(f32[2,8,256]{2,1,0:T(8,128)S(1)} %get-tuple-element.21), channel_id=1, source_target_pairs={{0,4},{4,0},{8,12},{12,8},{16,20},{20,16},{24,28},{28,24},{1,5},{5... | collective-permute-start | bytes 49160 | tf_op jit(solution)/shard_map/ppermute | solution.py:472
  16.4 3.5 %collective-permute-start.5 = (f32[11,8,256]{2,1,0:T(8,128)S(1)}, f32[11,8,256]{2,1,0:T(8,128)S(1)}, u32[]{:S(2)}, u32[]{:S(2)}) collective-permute-start(f32[11,8,256]{2,1,0:T(8,128)S(1)} %get-tuple-element.22), channel_id=1, source_target_pairs={{4,8},{8,4},{12,16},{16,12},{20,24},{24,20},{28,0},{0,28},{5,9},{9... | collective-permute-start | bytes 270344 | tf_op jit(solution)/shard_map/ppermute | solution.py:473
  20.0 0.0 collective-permute-done.7.inlet_b
  20.0 0.8 %collective-permute-done.6.inlet_a = f32[9,8,256]{2,1,0:T(8,128)S(1)} collective-permute-done((f32[9,8,256]{2,1,0:T(8,128)S(1)}, f32[9,8,256]{2,1,0:T(8,128)S(1)}, u32[]{:S(2)}, u32[]{:S(2)}) %collective-permute-start.6) | collective-permute-done | bytes 73760 | tf_op jit(solution)/shard_map/ppermute | solution.py:435
  20.8 2.2 %stream.1 = (f32[27,8,16,256]{3,2,1,0:T(8,128)}, f32[27,4,8,256]{3,2,1,0:T(8,128)}) custom-call(f32[27,8,16,256]{3,2,1,0:T(8,128)S(1)} %get-tuple-element.15.rel_main, f32[27,4,8,256]{3,2,1,0:T(8,128)S(1)} %get-tuple-element.16.rel_prec, f32[111,256]{1,0:T(8,128)S(1)} %collective-permute-done.2.recv_c, f32[111,256]{1,0:T(8,128)S(1)} %collective-permute-done.3.recv_d, ...), custom_call_target="tpu_custom_call" | custom-call | flops 1000000000 | bytes 1 | tf_op jit(solution)/shard_map/stream/pallas_call | solution.py:479
  23.0 0.0 collective-permute-done.1.recv_b
  23.0 0.0 collective-permute-done.4.corner_a
  23.0 0.6 %collective-permute-done.5.corner_b = f32[11,8,256]{2,1,0:T(8,128)S(1)} collective-permute-done((f32[11,8,256]{2,1,0:T(8,128)S(1)}, f32[11,8,256]{2,1,0:T(8,128)S(1)}, u32[]{:S(2)}, u32[]{:S(2)}) %collective-permute-start.5) | collective-permute-done | bytes 90144 | tf_op jit(solution)/shard_map/ppermute | solution.py:473
  23.6 0.9 %edges.1 = (f32[27,8,16,256]{3,2,1,0:T(8,128)}, f32[27,4,8,256]{3,2,1,0:T(8,128)}) custom-call(f32[27,8,16,256]{3,2,1,0:T(8,128)S(1)} %get-tuple-element.15.rel_main, f32[27,4,8,256]{3,2,1,0:T(8,128)S(1)} %get-tuple-element.16.rel_prec, f32[9,24,256]{2,1,0:T(8,128)S(1)} %collective-permute-done.recv_a, ...), custom_call_target="tpu_custom_call", output_to_operand_aliasing={{0}: (10, {}), {1}: (11, {})} | custom-call | tf_op jit(solution)/shard_map/edges/pallas_call | solution.py:493
  (2 shorter events, 0.0 us)
Async XLA Ops:
  5.4 3.1 %collective-permute-start.2 = (f32[111,256]{1,0:T(8,128)S(1)}, f32[111,256]{1,0:T(8,128)S(1)}, u32[]{:S(2)}, u32[]{:S(2)}) collective-permute-start(f32[111,256]{1,0:T(8,128)S(1)} %get-tuple-element.19), channel_id=1, source_target_pairs={{0,1},{1,0},{2,3},{3,2},{4,5},{5,4},{6,7},{7,6},{8,9},{9,8},{10,11... | collective-permute-start | bytes 341000 | tf_op jit(solution)/shard_map/ppermute | solution.py:437
  5.9 8.6 %collective-permute-start = (f32[9,24,256]{2,1,0:T(8,128)S(1)}, f32[9,24,256]{2,1,0:T(8,128)S(1)}, u32[]{:S(2)}, u32[]{:S(2)}) collective-permute-start(f32[9,24,256]{2,1,0:T(8,128)S(1)} %get-tuple-element.17), channel_id=1, source_target_pairs={{0,4},{4,0},{8,12},{12,8},{16,20},{20,16},{24,28},{28,24},{1,5},{5... | collective-permute-start | bytes 663560 | tf_op jit(solution)/shard_map/ppermute | solution.py:432
  8.5 6.0 %collective-permute-start.3 = (f32[111,256]{1,0:T(8,128)S(1)}, f32[111,256]{1,0:T(8,128)S(1)}, u32[]{:S(2)}, u32[]{:S(2)}) collective-permute-start(f32[111,256]{1,0:T(8,128)S(1)} %relay.1), channel_id=1, source_target_pairs={{1,2},{2,1},{3,0},{0,3},{5,6},{6,5},{7,4},{4,7},{9,10},{10,9},{11,... | collective-permute-start | bytes 341000 | tf_op jit(solution)/shard_map/ppermute | solution.py:461
  9.9 10.1 %collective-permute-start.7 = (f32[9,8,256]{2,1,0:T(8,128)S(1)}, f32[9,8,256]{2,1,0:T(8,128)S(1)}, u32[]{:S(2)}, u32[]{:S(2)}) collective-permute-start(f32[9,8,256]{2,1,0:T(8,128)S(1)} %get-tuple-element.23), channel_id=1, source_target_pairs={{28,2},{29,0},{30,3},{31,1}} | collective-permute-start | bytes 221192 | tf_op jit(solution)/shard_map/ppermute | solution.py:436
  11.2 9.6 %collective-permute-start.6 = (f32[9,8,256]{2,1,0:T(8,128)S(1)}, f32[9,8,256]{2,1,0:T(8,128)S(1)}, u32[]{:S(2)}, u32[]{:S(2)}) collective-permute-start(f32[9,8,256]{2,1,0:T(8,128)S(1)} %get-tuple-element.23), channel_id=1, source_target_pairs={{28,0},{29,2},{30,1},{31,3}} | collective-permute-start | bytes 221192 | tf_op jit(solution)/shard_map/ppermute | solution.py:435
  12.5 10.6 %collective-permute-start.1 = (f32[9,16,256]{2,1,0:T(8,128)S(1)}, f32[9,16,256]{2,1,0:T(8,128)S(1)}, u32[]{:S(2)}, u32[]{:S(2)}) collective-permute-start(f32[9,16,256]{2,1,0:T(8,128)S(1)} %get-tuple-element.18), channel_id=1, source_target_pairs={{4,8},{8,4},{12,16},{16,12},{20,24},{24,20},{5,9},{9,5},{13,17},{1... | collective-permute-start | bytes 442376 | tf_op jit(solution)/shard_map/ppermute | solution.py:434
  14.6 8.4 %collective-permute-start.4 = (f32[2,8,256]{2,1,0:T(8,128)S(1)}, f32[2,8,256]{2,1,0:T(8,128)S(1)}, u32[]{:S(2)}, u32[]{:S(2)}) collective-permute-start(f32[2,8,256]{2,1,0:T(8,128)S(1)} %get-tuple-element.21), channel_id=1, source_target_pairs={{0,4},{4,0},{8,12},{12,8},{16,20},{20,16},{24,28},{28,24},{1,5},{5... | collective-permute-start | bytes 49160 | tf_op jit(solution)/shard_map/ppermute | solution.py:472
  16.4 7.2 %collective-permute-start.5 = (f32[11,8,256]{2,1,0:T(8,128)S(1)}, f32[11,8,256]{2,1,0:T(8,128)S(1)}, u32[]{:S(2)}, u32[]{:S(2)}) collective-permute-start(f32[11,8,256]{2,1,0:T(8,128)S(1)} %get-tuple-element.22), channel_id=1, source_target_pairs={{4,8},{8,4},{12,16},{16,12},{20,24},{24,20},{28,0},{0,28},{5,9},{9... | collective-permute-start | bytes 270344 | tf_op jit(solution)/shard_map/ppermute | solution.py:473

commit v3 on v2

--- a/solution.py
+++ b/solution.py
@@ -1,3 +1,5 @@
+import functools
+
 import jax
 import jax.numpy as jnp
 import numpy as np
@@ -104,30 +106,60 @@
     return target
 
 
-def collide_kernel(
+def main_plane(main_in, cells_in, rel_main, keep, pull, slot, x):
+    extent_y, depth = main_in.shape[2:]
+    for y in range(0, extent_y, 8):
+        for z in range(0, depth, 128):
+            rows, lanes = pl.ds(y, 8), pl.ds(z, 128)
+            kind = cells_in[x, rows, lanes]
+            pops = [main_in[i, slot, rows, lanes] for i in range(27)]
+            relaxed = relaxed_tile(pops, keep, pull, kind == 2)
+            for i in range(27):
+                value = relaxed[i]
+                if z == 0:
+                    value = jnp.where(kind == 1, pops[26 - i], value)
+                rel_main[i, x, rows, lanes] = value
+
+
+def border_kernel(
     main_hbm, prec_hbm, cells_hbm, rates_ref,
-    rel_main, rel_prec, send_a, send_b, send_c, send_d, inlet_send,
-    main_in, prec_in, cells_in, in_sem, cell_sem,
+    cells_in, rel_main, rel_prec, send_a, send_b, send_c, send_d, inlet_send,
+    outer_in, prec_in, main_low, main_high, prec_low, prec_high, plane_sem, row_sem,
 ):
-    extent_x, extent_y, depth = main_in.shape[1:]
+    extent_x, extent_y, depth = rel_main.shape[1:]
     prec_x, prec_y = prec_in.shape[1:3]
+    planes = extent_x + prec_x
     odd_x = lax.rem(lax.axis_index("gx"), 2)
     odd_y = lax.rem(lax.axis_index("gy"), 2)
 
-    def fetch_main(x):
-        return pltpu.make_async_copy(main_hbm.at[:, x], main_in.at[:, x], in_sem.at[x])
+    def pick(odd, even_value, odd_value):
+        return jnp.where(odd == 0, even_value, odd_value)
 
     def fetch_prec(x):
-        return pltpu.make_async_copy(
-            prec_hbm.at[:, x], prec_in.at[:, x], in_sem.at[extent_x + x]
-        )
-
-    fetch_cells = pltpu.make_async_copy(cells_hbm, cells_in, cell_sem)
+        return pltpu.make_async_copy(prec_hbm.at[:, x], prec_in.at[:, x], plane_sem.at[3 + x])
+
+    def fetch_outer(k):
+        x = k * (extent_x - 1)
+        return pltpu.make_async_copy(main_hbm.at[:, x], outer_in.at[:, k], plane_sem.at[k])
+
+    fetch_cells = pltpu.make_async_copy(cells_hbm, cells_in, plane_sem.at[2])
+    rows = []
+    for hbm, low, high in ((main_hbm, main_low, main_high), (prec_hbm, prec_low, prec_high)):
+        for x in range(hbm.shape[1]):
+            for y, to in ((0, low), (hbm.shape[2] - 1, high)):
+                rows.append(
+                    pltpu.make_async_copy(
+                        hbm.at[:, x, pl.ds(y, 1), :], to.at[:, pl.ds(x, 1), :],
+                        row_sem.at[len(rows)],
+                    )
+                )
     for x in range(prec_x):
         fetch_prec(x).start()
     fetch_cells.start()
-    for x in range(extent_x):
-        fetch_main(x).start()
+    for k in range(2):
+        fetch_outer(k).start()
+    for copy in rows:
+        copy.start()
     keep, pull = moment_scales(rates_ref)
 
     def prec_plane(x, carry):
@@ -140,27 +172,15 @@
                     rel_prec[i, x, rows, lanes] = value
         return carry
 
-    def main_plane(x, carry):
-        fetch_main(x).wait()
-        for y in range(0, extent_y, 8):
-            for z in range(0, depth, 128):
-                rows, lanes = pl.ds(y, 8), pl.ds(z, 128)
-                kind = cells_in[x, rows, lanes]
-                pops = [main_in[i, x, rows, lanes] for i in range(27)]
-                for i, value in enumerate(relaxed_tile(pops, keep, pull, kind == 2)):
-                    if z == 0:
-                        value = jnp.where(kind == 1, main_in[26 - i, x, rows, lanes], value)
-                    rel_main[i, x, rows, lanes] = value
+    def outer_plane(k, carry):
+        fetch_outer(k).wait()
+        main_plane(outer_in, cells_in, rel_main, keep, pull, k, k * (extent_x - 1))
         return carry
 
     lax.fori_loop(0, prec_x, prec_plane, 0)
     fetch_cells.wait()
-    lax.fori_loop(0, extent_x, main_plane, 0)
-
-    def pick(odd, even_value, odd_value):
-        return jnp.where(odd == 0, even_value, odd_value)
-
-    planes = extent_x + prec_x
+    lax.fori_loop(0, 2, outer_plane, 0)
+
     for rel, first, size_x, size_y in (
         (rel_main, 0, extent_x, extent_y),
         (rel_prec, extent_y, prec_x, prec_y),
@@ -171,21 +191,60 @@
             if first == 0:
                 send_b[i] = pick(odd_x, low, high)
     inlet_send[...] = rel_prec[18:27, prec_x - 1]
-    for pair in range(9):
-        down, up = 9 * (pair // 3) + pair % 3, 9 * (pair // 3) + 6 + pair % 3
-        for rel, first, size_x, size_y in (
-            (rel_main, 0, extent_x, extent_y),
-            (rel_prec, extent_x, prec_x, prec_y),
-        ):
-            for x in range(size_x):
-                place = pl.ds(pair * planes + first + x, 1)
-                low, high = rel[down, x, 0:1, :], rel[up, x, size_y - 1 : size_y, :]
-                send_c[place, :] = pick(odd_y, high, low)
-                send_d[place, :] = pick(odd_y, low, high)
     for step in range(3):
         place = pl.ds(9 * planes + step, 1)
         first, last = outlet_rows(rel_prec, step)
         send_c[place, :] = pick(odd_y, first, last)
+
+    for copy in rows:
+        copy.wait()
+    for z in range(0, depth, 128):
+        lanes = pl.ds(z, 128)
+        for first, size_x, ends in (
+            (0, extent_x, ((main_low, 0), (main_high, extent_y - 1))),
+            (extent_x, prec_x, ((prec_low, None), (prec_high, None))),
+        ):
+            found = []
+            for ref, y in ends:
+                pops = [ref[i, :, lanes] for i in range(27)]
+                kind = None if y is None else cells_in[:, y, lanes]
+                disk = None if y is None else kind == 2
+                relaxed = relaxed_tile(pops, keep, pull, disk)
+                if y is not None and z == 0:
+                    relaxed = [
+                        jnp.where(kind == 1, pops[26 - i], relaxed[i]) for i in range(27)
+                    ]
+                found.append(relaxed)
+            for pair in range(9):
+                down, up = 9 * (pair // 3) + pair % 3, 9 * (pair // 3) + 6 + pair % 3
+                place = pl.ds(pair * planes + first, size_x)
+                low, high = found[0][down], found[1][up]
+                send_c[place, lanes] = pick(odd_y, high, low)
+                send_d[place, lanes] = pick(odd_y, low, high)
+
+
+def inner_kernel(at_start, main_hbm, cells_in, rates_hbm, rel_old, *rest):
+    rel_main, main_in, rates_ref, in_sem, rates_sem = rest[-6], *rest[-4:]
+
+    @pl.when((lax.axis_index("gx") == 0) == at_start)
+    def inner():
+        def fetch(x):
+            return pltpu.make_async_copy(main_hbm.at[:, x], main_in.at[:, x], in_sem.at[x])
+
+        extent_x = main_in.shape[1]
+        fetch_rates = pltpu.make_async_copy(rates_hbm, rates_ref, rates_sem)
+        fetch_rates.start()
+        for x in range(1, extent_x - 1):
+            fetch(x).start()
+        fetch_rates.wait()
+        keep, pull = moment_scales(rates_ref)
+
+        def plane(x, carry):
+            fetch(x).wait()
+            main_plane(main_in, cells_in, rel_main, keep, pull, x, x)
+            return carry
+
+        lax.fori_loop(1, extent_x - 1, plane, 0)
 
 
 def outlet_rows(rel_prec, step):
@@ -293,7 +352,7 @@
 
 
 def stream_kernel(
-    rel_main, rel_prec, recv_c, recv_d, inlet_a, inlet_b,
+    rel_main, rel_prec, recv_c, recv_d,
     main_out, prec_out, main_v, prec_v, out_sem,
 ):
     planes = rel_main.shape[1] + rel_prec.shape[1]
@@ -404,26 +463,54 @@
     params = pltpu.CompilerParams(vmem_limit_bytes=vmem_bytes)
     dma = pltpu.SemaphoreType.DMA
     block = (9, prec_y, depth)
-    main_rel, prec_rel, send_a, send_b, send_c, send_d, inlet_send = pl.pallas_call(
-        collide_kernel,
-        out_shape=tuple(
-            pltpu.VMEM(shape, f32)
-            for shape in (
-                main_pops.shape, prec_pops.shape, face, (9, extent_y, depth), side, side, block
-            )
+    main_row, prec_row = (27, extent_x, depth), (27, prec_x, depth)
+    cells_in, main_rel, prec_rel, send_a, send_b, send_c, send_d, inlet_send = pl.pallas_call(
+        border_kernel,
+        out_shape=(
+            pltpu.VMEM(cell_type.shape, jnp.int32),
+            *(
+                pltpu.VMEM(shape, f32)
+                for shape in (
+                    main_pops.shape, prec_pops.shape,
+                    face, (9, extent_y, depth), side, side, block,
+                )
+            ),
         ),
         in_specs=[any_space] * 3 + [smem_space],
-        out_specs=(vmem_space,) * 7,
+        out_specs=(vmem_space,) * 8,
         scratch_shapes=[
-            pltpu.VMEM(main_pops.shape, f32),
-            pltpu.VMEM(prec_pops.shape, f32),
-            pltpu.VMEM(cell_type.shape, jnp.int32),
-            dma((planes,)), dma(()),
+            *(
+                pltpu.VMEM(shape, f32)
+                for shape in (
+                    (27, 2, extent_y, depth), prec_pops.shape,
+                    main_row, main_row, prec_row, prec_row,
+                )
+            ),
+            dma((3 + prec_x,)), dma((2 * planes,)),
         ],
         compiler_params=params,
-        name="collide",
+        name="border",
     )(in_hbm(main_pops), in_hbm(prec_pops), in_hbm(cell_type), in_hbm(rates))
-    main_rel, prec_rel = in_vmem(main_rel), in_vmem(prec_rel)
+
+    def inner(at_start, name, rel, held, *awaited):
+        count = 4 + len(awaited)
+        return pl.pallas_call(
+            functools.partial(inner_kernel, at_start),
+            out_shape=(pltpu.VMEM(rel.shape, f32), pltpu.VMEM(held.shape, f32)),
+            in_specs=[any_space, vmem_space, any_space] + [vmem_space] * (count - 2),
+            out_specs=(vmem_space,) * 2,
+            scratch_shapes=[
+                pltpu.VMEM(main_pops.shape, f32),
+                pltpu.SMEM(rates.shape, f32),
+                dma((extent_x,)), dma(()),
+            ],
+            input_output_aliases={3: 0, count: 1},
+            compiler_params=params,
+            name=name,
+        )(in_hbm(main_pops), in_vmem(cells_in), in_hbm(rates), in_vmem(rel), *awaited, in_vmem(held))
+
+    main_rel, send_b = inner(True, "inner_first", main_rel, send_b)
+    prec_rel = in_vmem(prec_rel)
 
     half = count_y // 2
     base = (count_x - 1) * count_y
@@ -472,6 +559,8 @@
     corner_a = in_vmem(lax.ppermute(corner_a, "gx", swap_pairs(count_x, 0)))
     corner_b = in_vmem(lax.ppermute(corner_b, "gx", swap_pairs(count_x, 1)))
 
+    main_rel, prec_rel = inner(False, "inner_most", main_rel, prec_rel, inlet_a, inlet_b)
+    main_rel, prec_rel = in_vmem(main_rel), in_vmem(prec_rel)
     outs = (
         jax.ShapeDtypeStruct(main_pops.shape, f32),
         jax.ShapeDtypeStruct(prec_pops.shape, f32),
@@ -479,7 +568,7 @@
     main_part, prec_part = pl.pallas_call(
         stream_kernel,
         out_shape=outs,
-        in_specs=[vmem_space] * 6,
+        in_specs=[vmem_space] * 4,
         out_specs=(any_space, any_space),
         scratch_shapes=[
             pltpu.VMEM(main_pops.shape, f32),
@@ -489,7 +578,7 @@
         compiler_params=params,
         name="stream",
         cost_estimate=pl.CostEstimate(flops=10**9, bytes_accessed=1, transcendentals=0),
-    )(main_rel, prec_rel, recv_c, recv_d, inlet_a, inlet_b)
+    )(main_rel, prec_rel, recv_c, recv_d)
     main_next, prec_next = pl.pallas_call(
         edge_kernel,
         out_shape=outs,

time: 24.7 us -> 23.1 us (0.935)
  waiting for transfers between devices: 2.84 us -> 1.34 us
  starting transfers between devices: 13 us -> 12.1 us
  Pallas kernels: 7.95 us -> 8.74 us
    ppermute x1, waiting for transfers between devices: 1.41 us -> 0.01 us  [shards(): recv_a = in_vmem(lax.ppermute(send_a, 'gx', swap_pairs(count_x, 0)))]
    ppermute x1, starting transfers between devices: 1.82 us -> 0.84 us  [shards(): corner_a = in_vmem(lax.ppermute(corner_a, 'gx', swap_pairs(count_x, 0)))]
    pallas_call x2 -> x4, Pallas kernels: 7.01 us -> 7.8 us  [the longest x1 3.12 us: shards(): pl.pallas_call(border_kernel, out_shape=(pltpu.VMEM(cell_type.shape, jnp....]
  transfers between devices with their start and end apart: 8 -> 8, of which waited for: 3 -> 2; matrix products, arithmetic and copies ran while one was open for 0% -> 0% of each run, Pallas kernels for 9% -> 21%
where the time goes in v3:
time: 23.1 us; the launch traced here: 22.9 us
  starting transfers between devices  12.1 us (52%)
  Pallas kernels  8.74 us (38%)
  waiting for transfers between devices  1.34 us (6%)
  between operations  0.73 us (3%)
    ppermute x1, starting transfers between devices, shards(): corner_b = in_vmem(lax.ppermute(corner_b, 'gx', swap_pairs(count_x, 1)))  3.54 us
    pallas_call x1, Pallas kernels, shards(): pl.pallas_call(border_kernel, out_shape=(pltpu.VMEM(cell_type.shape, jnp....  3.12 us
    ppermute x1, starting transfers between devices, shards(): recv_a = in_vmem(lax.ppermute(send_a, 'gx', swap_pairs(count_x, 0)))  2.59 us
    pallas_call x2, Pallas kernels, inner(): pl.pallas_call(functools.partial(inner_kernel, at_start), out_shape=(pltp...  2.45 us
    pallas_call x1, Pallas kernels, shards(): pl.pallas_call(stream_kernel, out_shape=outs, in_specs=[vmem_space] * 4,...  2.23 us
    ppermute x1, starting transfers between devices, shards(): recv_d = in_vmem(lax.ppermute(send_d, 'gy', swap_pairs(count_y, 1)))  1.33 us
    ppermute x1, starting transfers between devices, shards(): inlet_a = in_vmem(lax.ppermute(inlet_send, ('gx', 'gy'), near))  1.29 us
    ppermute x1, starting transfers between devices, shards(): inlet_b = in_vmem(lax.ppermute(inlet_send, ('gx', 'gy'), far))  1.28 us
  transfers between devices with their start and end apart: 8, of which 2 were waited for; matrix products, arithmetic and copies ran while one was open for 0% of the time, Pallas kernels for 21%

profile of v3, /device:TPU:0, one launch (start us, length us, event | category | flops | bytes accessed | tf_op | source)
XLA Modules:
  0.0 22.9 jit_solution(12665336259692046051)
XLA Ops:
  0.6 3.1 %border.1 = (s32[8,16,256]{2,1,0:T(8,128)S(1)}, f32[27,8,16,256]{3,2,1,0:T(8,128)S(1)}, f32[27,4,8,256]{3,2,1,0:T(8,128)S(1)}, f32[9,24,256]{2,1,0:T(8,128)S(1)}...) custom-call(f32[27,8,16,256]{3,2,1,0:T(8,128)} %main_hbm.5, ...), custom_call_target="tpu_custom_call" | custom-call | tf_op jit(solution)/shard_map/border/pallas_call | solution.py:467
  3.8 0.5 %collective-permute-start.4 = (f32[111,256]{1,0:T(8,128)S(1)}, f32[111,256]{1,0:T(8,128)S(1)}, u32[]{:S(2)}, u32[]{:S(2)}) collective-permute-start(f32[111,256]{1,0:T(8,128)S(1)} %get-tuple-element.30), channel_id=1, source_target_pairs={{0,1},{1,0},{2,3},{3,2},{4,5},{5,4},{6,7},{7,6},{8,9},{9,8},{10,11... | collective-permute-start | bytes 341000 | tf_op jit(solution)/shard_map/ppermute | solution.py:524
  4.3 2.6 %collective-permute-start.2 = (f32[9,24,256]{2,1,0:T(8,128)S(1)}, f32[9,24,256]{2,1,0:T(8,128)S(1)}, u32[]{:S(2)}, u32[]{:S(2)}) collective-permute-start(f32[9,24,256]{2,1,0:T(8,128)S(1)} %get-tuple-element.28), channel_id=1, source_target_pairs={{0,4},{4,0},{8,12},{12,8},{16,20},{20,16},{24,28},{28,24},{1,5},{5... | collective-permute-start | bytes 663560 | tf_op jit(solution)/shard_map/ppermute | solution.py:519
  6.9 0.0 collective-permute-done.4.recv_c
  6.9 1.3 %collective-permute-start.5 = (f32[111,256]{1,0:T(8,128)S(1)}, f32[111,256]{1,0:T(8,128)S(1)}, u32[]{:S(2)}, u32[]{:S(2)}) collective-permute-start(f32[111,256]{1,0:T(8,128)S(1)} %relay.1), channel_id=1, source_target_pairs={{1,2},{2,1},{3,0},{0,3},{5,6},{6,5},{7,4},{4,7},{9,10},{10,9},{11,... | collective-permute-start | bytes 341000 | tf_op jit(solution)/shard_map/ppermute | solution.py:548
  8.2 1.3 %collective-permute-start.1 = (f32[9,8,256]{2,1,0:T(8,128)S(1)}, f32[9,8,256]{2,1,0:T(8,128)S(1)}, u32[]{:S(2)}, u32[]{:S(2)}) collective-permute-start(f32[9,8,256]{2,1,0:T(8,128)S(1)} %get-tuple-element.24), channel_id=1, source_target_pairs={{28,2},{29,0},{30,3},{31,1}} | collective-permute-start | bytes 221192 | tf_op jit(solution)/shard_map/ppermute | solution.py:523
  9.5 1.3 %collective-permute-start = (f32[9,8,256]{2,1,0:T(8,128)S(1)}, f32[9,8,256]{2,1,0:T(8,128)S(1)}, u32[]{:S(2)}, u32[]{:S(2)}) collective-permute-start(f32[9,8,256]{2,1,0:T(8,128)S(1)} %get-tuple-element.24), channel_id=1, source_target_pairs={{28,0},{29,2},{30,1},{31,3}} | collective-permute-start | bytes 221192 | tf_op jit(solution)/shard_map/ppermute | solution.py:522
  10.8 2.4 %inner_first.1 = (f32[27,8,16,256]{3,2,1,0:T(8,128)S(1)}, f32[9,16,256]{2,1,0:T(8,128)S(1)}) custom-call(f32[27,8,16,256]{3,2,1,0:T(8,128)} %main_hbm.5, s32[8,16,256]{2,1,0:T(8,128)S(1)} %get-tuple-element.20.cells_in, f32[27]{0:T(128)} %rates_hbm.3, ...), custom_call_target="tpu_custom_call", output_to_operand_aliasing={{0}: (3, {}), {1}: (4, {})} | custom-call | tf_op jit(solution)/shard_map/inner_first/pallas_call | solution.py:497
  13.2 0.7 %collective-permute-start.3 = (f32[9,16,256]{2,1,0:T(8,128)S(1)}, f32[9,16,256]{2,1,0:T(8,128)S(1)}, u32[]{:S(2)}, u32[]{:S(2)}) collective-permute-start(f32[9,16,256]{2,1,0:T(8,128)S(1)} %get-tuple-element.29), channel_id=1, source_target_pairs={{4,8},{8,4},{12,16},{16,12},{20,24},{24,20},{5,9},{9,5},{13,17},{1... | collective-permute-start | bytes 442376 | tf_op jit(solution)/shard_map/ppermute | solution.py:521
  13.9 0.0 collective-permute-done.2.recv_a
  13.9 0.0 collective-permute-done.5.recv_d
  13.9 0.8 %collective-permute-start.6 = (f32[2,8,256]{2,1,0:T(8,128)S(1)}, f32[2,8,256]{2,1,0:T(8,128)S(1)}, u32[]{:S(2)}, u32[]{:S(2)}) collective-permute-start(f32[2,8,256]{2,1,0:T(8,128)S(1)} %get-tuple-element.32), channel_id=1, source_target_pairs={{0,4},{4,0},{8,12},{12,8},{16,20},{20,16},{24,28},{28,24},{1,5},{5... | collective-permute-start | bytes 49160 | tf_op jit(solution)/shard_map/ppermute | solution.py:559
  14.8 3.5 %collective-permute-start.7 = (f32[11,8,256]{2,1,0:T(8,128)S(1)}, f32[11,8,256]{2,1,0:T(8,128)S(1)}, u32[]{:S(2)}, u32[]{:S(2)}) collective-permute-start(f32[11,8,256]{2,1,0:T(8,128)S(1)} %get-tuple-element.33), channel_id=1, source_target_pairs={{4,8},{8,4},{12,16},{16,12},{20,24},{24,20},{28,0},{0,28},{5,9},{9... | collective-permute-start | bytes 270344 | tf_op jit(solution)/shard_map/ppermute | solution.py:560
  18.3 0.0 collective-permute-done.1.rest_1_.inlet_b
  18.3 0.8 %collective-permute-done.rest_0_.inlet_a = f32[9,8,256]{2,1,0:T(8,128)S(1)} collective-permute-done((f32[9,8,256]{2,1,0:T(8,128)S(1)}, f32[9,8,256]{2,1,0:T(8,128)S(1)}, u32[]{:S(2)}, u32[]{:S(2)}) %collective-permute-start) | collective-permute-done | bytes 73760 | tf_op jit(solution)/shard_map/ppermute | solution.py:522
  19.1 0.1 inner_most.1
  19.2 2.2 %stream.1 = (f32[27,8,16,256]{3,2,1,0:T(8,128)}, f32[27,4,8,256]{3,2,1,0:T(8,128)}) custom-call(f32[27,8,16,256]{3,2,1,0:T(8,128)S(1)} %get-tuple-element.26.rel_main, f32[27,4,8,256]{3,2,1,0:T(8,128)S(1)} %get-tuple-element.27.rel_prec, f32[111,256]{1,0:T(8,128)S(1)} %collective-permute-done.4.recv_c, f32[111,256]{1,0:T(8,128)S(1)} %collective-permute-done.5.recv_d), custom_call_target="tpu_custom_call" | custom-call | flops 1000000000 | bytes 1 | tf_op jit(solution)/shard_map/stream/pallas_call | solution.py:568
  21.5 0.0 collective-permute-done.3.recv_b
  21.5 0.0 collective-permute-done.6.corner_a
  21.5 0.5 %collective-permute-done.7.corner_b = f32[11,8,256]{2,1,0:T(8,128)S(1)} collective-permute-done((f32[11,8,256]{2,1,0:T(8,128)S(1)}, f32[11,8,256]{2,1,0:T(8,128)S(1)}, u32[]{:S(2)}, u32[]{:S(2)}) %collective-permute-start.7) | collective-permute-done | bytes 90144 | tf_op jit(solution)/shard_map/ppermute | solution.py:560
  22.0 0.9 %edges.1 = (f32[27,8,16,256]{3,2,1,0:T(8,128)}, f32[27,4,8,256]{3,2,1,0:T(8,128)}) custom-call(f32[27,8,16,256]{3,2,1,0:T(8,128)S(1)} %get-tuple-element.26.rel_main, f32[27,4,8,256]{3,2,1,0:T(8,128)S(1)} %get-tuple-element.27.rel_prec, f32[9,24,256]{2,1,0:T(8,128)S(1)} %collective-permute-done.2.recv_a, ...), custom_call_target="tpu_custom_call", output_to_operand_aliasing={{0}: (10, {}), {1}: (11, {})} | custom-call | tf_op jit(solution)/shard_map/edges/pallas_call | solution.py:582
  (2 shorter events, 0.0 us)
Async XLA Ops:
  3.8 3.1 %collective-permute-start.4 = (f32[111,256]{1,0:T(8,128)S(1)}, f32[111,256]{1,0:T(8,128)S(1)}, u32[]{:S(2)}, u32[]{:S(2)}) collective-permute-start(f32[111,256]{1,0:T(8,128)S(1)} %get-tuple-element.30), channel_id=1, source_target_pairs={{0,1},{1,0},{2,3},{3,2},{4,5},{5,4},{6,7},{7,6},{8,9},{9,8},{10,11... | collective-permute-start | bytes 341000 | tf_op jit(solution)/shard_map/ppermute | solution.py:524
  4.3 9.6 %collective-permute-start.2 = (f32[9,24,256]{2,1,0:T(8,128)S(1)}, f32[9,24,256]{2,1,0:T(8,128)S(1)}, u32[]{:S(2)}, u32[]{:S(2)}) collective-permute-start(f32[9,24,256]{2,1,0:T(8,128)S(1)} %get-tuple-element.28), channel_id=1, source_target_pairs={{0,4},{4,0},{8,12},{12,8},{16,20},{20,16},{24,28},{28,24},{1,5},{5... | collective-permute-start | bytes 663560 | tf_op jit(solution)/shard_map/ppermute | solution.py:519
  6.9 7.0 %collective-permute-start.5 = (f32[111,256]{1,0:T(8,128)S(1)}, f32[111,256]{1,0:T(8,128)S(1)}, u32[]{:S(2)}, u32[]{:S(2)}) collective-permute-start(f32[111,256]{1,0:T(8,128)S(1)} %relay.1), channel_id=1, source_target_pairs={{1,2},{2,1},{3,0},{0,3},{5,6},{6,5},{7,4},{4,7},{9,10},{10,9},{11,... | collective-permute-start | bytes 341000 | tf_op jit(solution)/shard_map/ppermute | solution.py:548
  8.2 10.1 %collective-permute-start.1 = (f32[9,8,256]{2,1,0:T(8,128)S(1)}, f32[9,8,256]{2,1,0:T(8,128)S(1)}, u32[]{:S(2)}, u32[]{:S(2)}) collective-permute-start(f32[9,8,256]{2,1,0:T(8,128)S(1)} %get-tuple-element.24), channel_id=1, source_target_pairs={{28,2},{29,0},{30,3},{31,1}} | collective-permute-start | bytes 221192 | tf_op jit(solution)/shard_map/ppermute | solution.py:523
  9.5 9.6 %collective-permute-start = (f32[9,8,256]{2,1,0:T(8,128)S(1)}, f32[9,8,256]{2,1,0:T(8,128)S(1)}, u32[]{:S(2)}, u32[]{:S(2)}) collective-permute-start(f32[9,8,256]{2,1,0:T(8,128)S(1)} %get-tuple-element.24), channel_id=1, source_target_pairs={{28,0},{29,2},{30,1},{31,3}} | collective-permute-start | bytes 221192 | tf_op jit(solution)/shard_map/ppermute | solution.py:522
  13.2 8.3 %collective-permute-start.3 = (f32[9,16,256]{2,1,0:T(8,128)S(1)}, f32[9,16,256]{2,1,0:T(8,128)S(1)}, u32[]{:S(2)}, u32[]{:S(2)}) collective-permute-start(f32[9,16,256]{2,1,0:T(8,128)S(1)} %get-tuple-element.29), channel_id=1, source_target_pairs={{4,8},{8,4},{12,16},{16,12},{20,24},{24,20},{5,9},{9,5},{13,17},{1... | collective-permute-start | bytes 442376 | tf_op jit(solution)/shard_map/ppermute | solution.py:521
  13.9 7.6 %collective-permute-start.6 = (f32[2,8,256]{2,1,0:T(8,128)S(1)}, f32[2,8,256]{2,1,0:T(8,128)S(1)}, u32[]{:S(2)}, u32[]{:S(2)}) collective-permute-start(f32[2,8,256]{2,1,0:T(8,128)S(1)} %get-tuple-element.32), channel_id=1, source_target_pairs={{0,4},{4,0},{8,12},{12,8},{16,20},{20,16},{24,28},{28,24},{1,5},{5... | collective-permute-start | bytes 49160 | tf_op jit(solution)/shard_map/ppermute | solution.py:559
  14.8 7.2 %collective-permute-start.7 = (f32[11,8,256]{2,1,0:T(8,128)S(1)}, f32[11,8,256]{2,1,0:T(8,128)S(1)}, u32[]{:S(2)}, u32[]{:S(2)}) collective-permute-start(f32[11,8,256]{2,1,0:T(8,128)S(1)} %get-tuple-element.33), channel_id=1, source_target_pairs={{4,8},{8,4},{12,16},{16,12},{20,24},{24,20},{28,0},{0,28},{5,9},{9... | collective-permute-start | bytes 270344 | tf_op jit(solution)/shard_map/ppermute | solution.py:560

commit v4 on v3

--- a/solution.py
+++ b/solution.py
@@ -9,7 +9,7 @@
 from jax.sharding import PartitionSpec as P
 
 drag_scale = -0.5 * 0.75
-vmem_bytes = 20 * 1024 * 1024
+vmem_bytes = 24 * 1024 * 1024
 any_space = pl.BlockSpec(memory_space=pltpu.HBM)
 vmem_space = pl.BlockSpec(memory_space=pltpu.VMEM)
 smem_space = pl.BlockSpec(memory_space=pltpu.SMEM)
@@ -123,7 +123,7 @@
 
 def border_kernel(
     main_hbm, prec_hbm, cells_hbm, rates_ref,
-    cells_in, rel_main, rel_prec, send_a, send_b, send_c, send_d, inlet_send,
+    cells_in, rel_main, rel_prec, send_a, send_b, send_c, send_d,
     outer_in, prec_in, main_low, main_high, prec_low, prec_high, plane_sem, row_sem,
 ):
     extent_x, extent_y, depth = rel_main.shape[1:]
@@ -190,7 +190,8 @@
             send_a[i, first : first + size_y] = pick(odd_x, high, low)
             if first == 0:
                 send_b[i] = pick(odd_x, low, high)
-    inlet_send[...] = rel_prec[18:27, prec_x - 1]
+    for i in range(9):
+        send_c[pl.ds(9 * planes + 4 + i * prec_y, prec_y), :] = rel_prec[18 + i, prec_x - 1]
     for step in range(3):
         place = pl.ds(9 * planes + step, 1)
         first, last = outlet_rows(rel_prec, step)
@@ -223,28 +224,37 @@
                 send_d[place, lanes] = pick(odd_y, low, high)
 
 
-def inner_kernel(at_start, main_hbm, cells_in, rates_hbm, rel_old, *rest):
-    rel_main, main_in, rates_ref, in_sem, rates_sem = rest[-6], *rest[-4:]
-
-    @pl.when((lax.axis_index("gx") == 0) == at_start)
+def inner_planes(
+    main_hbm, cells_in, rates_hbm, rel_main, main_in, rates_ref, in_sem, rates_sem
+):
+    def fetch(x):
+        return pltpu.make_async_copy(main_hbm.at[:, x], main_in.at[:, x], in_sem.at[x])
+
+    extent_x = main_in.shape[1]
+    fetch_rates = pltpu.make_async_copy(rates_hbm, rates_ref, rates_sem)
+    fetch_rates.start()
+    for x in range(1, extent_x - 1):
+        fetch(x).start()
+    fetch_rates.wait()
+    keep, pull = moment_scales(rates_ref)
+
+    def plane(x, carry):
+        fetch(x).wait()
+        main_plane(main_in, cells_in, rel_main, keep, pull, x, x)
+        return carry
+
+    lax.fori_loop(1, extent_x - 1, plane, 0)
+
+
+def first_kernel(
+    main_hbm, cells_in, rates_hbm, rel_old, held_old,
+    rel_main, held, main_in, rates_ref, in_sem, rates_sem,
+):
+    @pl.when(lax.axis_index("gx") == 0)
     def inner():
-        def fetch(x):
-            return pltpu.make_async_copy(main_hbm.at[:, x], main_in.at[:, x], in_sem.at[x])
-
-        extent_x = main_in.shape[1]
-        fetch_rates = pltpu.make_async_copy(rates_hbm, rates_ref, rates_sem)
-        fetch_rates.start()
-        for x in range(1, extent_x - 1):
-            fetch(x).start()
-        fetch_rates.wait()
-        keep, pull = moment_scales(rates_ref)
-
-        def plane(x, carry):
-            fetch(x).wait()
-            main_plane(main_in, cells_in, rel_main, keep, pull, x, x)
-            return carry
-
-        lax.fori_loop(1, extent_x - 1, plane, 0)
+        inner_planes(
+            main_hbm, cells_in, rates_hbm, rel_main, main_in, rates_ref, in_sem, rates_sem
+        )
 
 
 def outlet_rows(rel_prec, step):
@@ -253,12 +263,19 @@
     return first, rel_prec[24 + step, prec_x - 1, prec_y - 1 : prec_y, :]
 
 
-def relay_kernel(send_d, recv_c, relayed_d):
-    own = recv_c.shape[0] // 9 * 9
+def relay_kernel(rel_prec, send_d, recv_c, relayed_d, pair_send):
+    prec_x, prec_y = rel_prec.shape[1:3]
+    own = send_d.shape[0] // 9 * 9
     relayed_d[0:own] = send_d[0:own]
-    for step in range(recv_c.shape[0] - own):
+    for step in range(send_d.shape[0] - own):
         place = pl.ds(own + step, 1)
         relayed_d[place, :] = recv_c[place, :]
+    odd_y = lax.rem(lax.axis_index("gy"), 2)
+    for i in range(9):
+        mine = rel_prec[18 + i, prec_x - 1]
+        other = recv_c[pl.ds(own + 4 + i * prec_y, prec_y), :]
+        pair_send[0, i] = jnp.where(odd_y == 0, mine, other)
+        pair_send[1, i] = jnp.where(odd_y == 0, other, mine)
 
 
 def own_rows_kernel(rel_prec, own_rows):
@@ -274,10 +291,10 @@
     return jnp.where(odd_y == 0, other, one), jnp.where(odd_y == 0, one, other)
 
 
-def corner_kernel(rel_prec, recv_a, recv_c, recv_d, *rest):
+def corner_kernel(rel_prec, recv_c, recv_d, *rest):
     fetched, (corner_a, corner_b) = rest[:-2], rest[-2:]
     prec_x, prec_y = rel_prec.shape[1:3]
-    planes = recv_c.shape[0] // 9
+    planes = recv_d.shape[0] // 9
     extent_x = planes - prec_x
     place_x, place_y = lax.axis_index("gx"), lax.axis_index("gy")
     count_y = lax.axis_size("gy")
@@ -351,9 +368,8 @@
     return jnp.where(from_low == 1, recv_c[where, :], recv_d[where, :])
 
 
-def stream_kernel(
-    rel_main, rel_prec, recv_c, recv_d,
-    main_out, prec_out, main_v, prec_v, out_sem,
+def stream_planes(
+    rel_main, rel_prec, recv_c, recv_d, main_out, prec_out, main_v, prec_v, out_sem,
 ):
     planes = rel_main.shape[1] + rel_prec.shape[1]
     copies = []
@@ -394,61 +410,114 @@
         copy.wait()
 
 
-def edge_kernel(
-    rel_main, rel_prec, recv_a, recv_b, recv_c, recv_d, corner_a, corner_b, inlet_a, inlet_b,
-    main_old, prec_old, main_out, prec_out, main_v, prec_v, out_sem,
-):
-    extent_x, extent_y, _ = rel_main.shape[1:]
-    prec_x, prec_y = rel_prec.shape[1:3]
-    planes = extent_x + prec_x
-    place_x, place_y = lax.axis_index("gx"), lax.axis_index("gy")
-    count_x, count_y = lax.axis_size("gx"), lax.axis_size("gy")
-    odd_x = lax.rem(place_x, 2)
-    at_first, at_last = place_x == 0, place_x == count_x - 1
-    near = place_y < count_y // 2
+def middle_kernel(
+    main_hbm, cells_in, rates_hbm, rel_old, rel_prec, recv_c, recv_d, recv_a, inlet,
+    rel_main, main_out, prec_out,
+    main_in, rates_ref, main_v, prec_v, in_sem, rates_sem, out_sem,
+):
+    @pl.when(lax.axis_index("gx") != 0)
+    def inner():
+        inner_planes(
+            main_hbm, cells_in, rates_hbm, rel_main, main_in, rates_ref, in_sem, rates_sem
+        )
+
+    @pl.when(lax.axis_index("gx") == 0)
+    def stream():
+        stream_planes(
+            rel_main, rel_prec, recv_c, recv_d, main_out, prec_out, main_v, prec_v, out_sem
+        )
+
+
+def stream_kernel(
+    rel_main, rel_prec, recv_c, recv_d, inlet, main_old, prec_old,
+    main_out, prec_out, main_v, prec_v, out_sem,
+):
+    @pl.when(lax.axis_index("gx") != 0)
+    def stream():
+        stream_planes(
+            rel_main, rel_prec, recv_c, recv_d, main_out, prec_out, main_v, prec_v, out_sem
+        )
+
+
+def patch_side(low_side, rel_main, rel_prec, faces, out_refs, stages, out_sem):
     copies = []
-    for rel, out_v, out_hbm, lattice in (
-        (rel_prec, prec_v, prec_out, 1),
-        (rel_main, main_v, main_out, 0),
-    ):
-        size_x, size_y = rel.shape[1:3]
-        start_y = extent_y if lattice else 0
-        for low_side in (True, False):
-            x = 0 if low_side else size_x - 1
-            from_one = odd_x if low_side else 1 - odd_x
-            for part in range(9):
-                i = part + (18 if low_side else 0)
-                step_y, step_z = digits(i)[1] - 1, digits(i)[2] - 1
-                rows = pl.ds(start_y, size_y)
-                other = corner_b[part] if lattice else recv_b[part]
-                value = jnp.where(from_one == 1, recv_a[part, rows], other)
-                halo = None
-                if step_y:
-                    where = pl.ds((0 if step_y == 1 else 3) + step_z + 1, 1)
-                    halo = jnp.where(
-                        from_one == 1, corner_a[lattice, where, :], corner_b[9 + lattice, where, :]
-                    )
-                if not lattice and low_side:
-                    lower = jnp.where(near, inlet_a[part], inlet_b[part])
-                    upper = jnp.where(near, inlet_b[part], inlet_a[part])
-                    whole = jnp.concatenate([lower, upper], axis=0)
-                    value = jnp.where(at_first, whole, value)
-                if not lattice and not low_side:
-                    value = jnp.where(at_last, rel[i, size_x - 1], value)
-                    if step_y:
-                        row = side_row(recv_c, recv_d, i, size_x - 1, planes)
-                        halo = jnp.where(at_last, row, halo)
-                out_v[part, 0 if low_side else 1] = streamed(i, x, rel, value, halo)
-            first = 18 if low_side else 0
-            copy = pltpu.make_async_copy(
-                out_v.at[:, 0 if low_side else 1],
-                out_hbm.at[first : first + 9, x],
-                out_sem.at[2 * lattice + (0 if low_side else 1)],
+    for lattice in (1, 0):
+        rel, out_v = (rel_main, rel_prec)[lattice], stages[lattice]
+        x = 0 if low_side else rel.shape[1] - 1
+        first = 18 if low_side else 0
+        for part in range(9):
+            value, halo = faces(lattice, low_side, part)
+            out_v[part] = streamed(part + first, x, rel, value, halo)
+        copies.append(
+            pltpu.make_async_copy(
+                out_v, out_refs[lattice].at[first : first + 9, x], out_sem.at[lattice]
             )
-            copy.start()
-            copies.append(copy)
+        )
+        copies[-1].start()
     for copy in copies:
         copy.wait()
+
+
+def face_row(part):
+    step_y, step_z = part // 3 - 1, part % 3 - 1
+    return (0 if step_y == 1 else 3) + step_z + 1 if step_y else None
+
+
+def even_edge_kernel(
+    rel_main, rel_prec, recv_a, corner_a, main_old, prec_old,
+    main_out, prec_out, main_v, prec_v, out_sem,
+):
+    odd_x = lax.rem(lax.axis_index("gx"), 2)
+
+    def faces(lattice, low_side, part):
+        start, size = ((0, main_v.shape[1]), (main_v.shape[1], prec_v.shape[1]))[lattice]
+        row = face_row(part)
+        halo = None if row is None else corner_a[lattice, row : row + 1, :]
+        return recv_a[part, start : start + size], halo
+
+    for low_side in (True, False):
+
+        @pl.when(odd_x == (1 if low_side else 0))
+        def patch(low_side=low_side):
+            patch_side(
+                low_side, rel_main, rel_prec, faces,
+                (main_out, prec_out), (main_v, prec_v), out_sem,
+            )
+
+
+def odd_edge_kernel(
+    rel_main, rel_prec, recv_b, recv_c, recv_d, corner_b, inlet, main_old, prec_old,
+    main_out, prec_out, main_v, prec_v, out_sem,
+):
+    extent_x = rel_main.shape[1]
+    planes = extent_x + rel_prec.shape[1]
+    place_x = lax.axis_index("gx")
+    odd_x = lax.rem(place_x, 2)
+    at_first, at_last = place_x == 0, place_x == lax.axis_size("gx") - 1
+
+    def faces(lattice, low_side, part):
+        row = face_row(part)
+        halo = None if row is None else corner_b[9 + lattice, row : row + 1, :]
+        if lattice:
+            return corner_b[part], halo
+        value = recv_b[part]
+        if low_side:
+            whole = jnp.concatenate([inlet[0, part], inlet[1, part]], axis=0)
+            return jnp.where(at_first, whole, value), halo
+        value = jnp.where(at_last, rel_main[part, extent_x - 1], value)
+        if row is not None:
+            own = side_row(recv_c, recv_d, part, extent_x - 1, planes)
+            halo = jnp.where(at_last, own, halo)
+        return value, halo
+
+    for low_side in (True, False):
+
+        @pl.when(odd_x == (0 if low_side else 1))
+        def patch(low_side=low_side):
+            patch_side(
+                low_side, rel_main, rel_prec, faces,
+                (main_out, prec_out), (main_v, prec_v), out_sem,
+            )
 
 
 def shards(prec_pops, main_pops, cell_type, rates):
@@ -460,11 +529,11 @@
     f32 = jnp.float32
     face = (9, extent_y + prec_y, depth)
     side = (9 * planes + 3, depth)
+    side_outlet = (9 * planes + 4 + 9 * prec_y, depth)
     params = pltpu.CompilerParams(vmem_limit_bytes=vmem_bytes)
     dma = pltpu.SemaphoreType.DMA
-    block = (9, prec_y, depth)
     main_row, prec_row = (27, extent_x, depth), (27, prec_x, depth)
-    cells_in, main_rel, prec_rel, send_a, send_b, send_c, send_d, inlet_send = pl.pallas_call(
+    cells_in, main_rel, prec_rel, send_a, send_b, send_c, send_d = pl.pallas_call(
         border_kernel,
         out_shape=(
             pltpu.VMEM(cell_type.shape, jnp.int32),
@@ -472,12 +541,12 @@
                 pltpu.VMEM(shape, f32)
                 for shape in (
                     main_pops.shape, prec_pops.shape,
-                    face, (9, extent_y, depth), side, side, block,
+                    face, (9, extent_y, depth), side_outlet, side,
                 )
             ),
         ),
         in_specs=[any_space] * 3 + [smem_space],
-        out_specs=(vmem_space,) * 8,
+        out_specs=(vmem_space,) * 7,
         scratch_shapes=[
             *(
                 pltpu.VMEM(shape, f32)
@@ -491,48 +560,40 @@
         compiler_params=params,
         name="border",
     )(in_hbm(main_pops), in_hbm(prec_pops), in_hbm(cell_type), in_hbm(rates))
-
-    def inner(at_start, name, rel, held, *awaited):
-        count = 4 + len(awaited)
-        return pl.pallas_call(
-            functools.partial(inner_kernel, at_start),
-            out_shape=(pltpu.VMEM(rel.shape, f32), pltpu.VMEM(held.shape, f32)),
-            in_specs=[any_space, vmem_space, any_space] + [vmem_space] * (count - 2),
-            out_specs=(vmem_space,) * 2,
-            scratch_shapes=[
-                pltpu.VMEM(main_pops.shape, f32),
-                pltpu.SMEM(rates.shape, f32),
-                dma((extent_x,)), dma(()),
-            ],
-            input_output_aliases={3: 0, count: 1},
-            compiler_params=params,
-            name=name,
-        )(in_hbm(main_pops), in_vmem(cells_in), in_hbm(rates), in_vmem(rel), *awaited, in_vmem(held))
-
-    main_rel, send_b = inner(True, "inner_first", main_rel, send_b)
+    long_run = pl.CostEstimate(flops=10**9, bytes_accessed=1, transcendentals=0)
+    inner_scratch = [pltpu.VMEM(main_pops.shape, f32), pltpu.SMEM(rates.shape, f32)]
+    inner_given = in_hbm(main_pops), in_vmem(cells_in), in_hbm(rates)
+    main_rel, send_b = pl.pallas_call(
+        first_kernel,
+        out_shape=(pltpu.VMEM(main_pops.shape, f32), pltpu.VMEM(send_b.shape, f32)),
+        in_specs=[any_space, vmem_space, any_space] + [vmem_space] * 2,
+        out_specs=(vmem_space,) * 2,
+        scratch_shapes=inner_scratch + [dma((extent_x,)), dma(())],
+        input_output_aliases={3: 0, 4: 1},
+        cost_estimate=long_run,
+        compiler_params=params,
+        name="inner_first",
+    )(*inner_given, in_vmem(main_rel), in_vmem(send_b))
     prec_rel = in_vmem(prec_rel)
 
     half = count_y // 2
     base = (count_x - 1) * count_y
-    near = [(base + s, s // 2 + half * (s % 2)) for s in range(count_y)]
-    far = [(base + s, s // 2 + half * (1 - s % 2)) for s in range(count_y)]
+    to_inlet = [(base + s, s // 2 + half * (s % 2)) for s in range(count_y)]
     recv_a = in_vmem(lax.ppermute(send_a, "gx", swap_pairs(count_x, 0)))
     across = [p for p in swap_pairs(count_x, 1) if abs(p[0] - p[1]) == 1]
     recv_b = in_vmem(lax.ppermute(send_b, "gx", across))
-    inlet_a = in_vmem(lax.ppermute(inlet_send, ("gx", "gy"), near))
-    inlet_b = in_vmem(lax.ppermute(inlet_send, ("gx", "gy"), far))
     recv_c = in_vmem(lax.ppermute(send_c, "gy", swap_pairs(count_y, 0)))
+    send_d, pair_send = pl.pallas_call(
+        relay_kernel,
+        out_shape=(pltpu.VMEM(side, f32), pltpu.VMEM((2, 9, prec_y, depth), f32)),
+        in_specs=[vmem_space] * 3,
+        out_specs=(vmem_space,) * 2,
+        compiler_params=params,
+        name="relay",
+    )(prec_rel, in_vmem(send_d), recv_c)
+    inlet = in_vmem(lax.ppermute(pair_send, ("gx", "gy"), to_inlet))
     fetched = []
-    if count_y == 4:
-        send_d = pl.pallas_call(
-            relay_kernel,
-            out_shape=pltpu.VMEM(side, f32),
-            in_specs=[vmem_space] * 2,
-            out_specs=vmem_space,
-            compiler_params=params,
-            name="relay",
-        )(in_vmem(send_d), recv_c)
-    else:
+    if count_y != 4:
         own_rows = pl.pallas_call(
             own_rows_kernel,
             out_shape=pltpu.VMEM((8, depth), f32),
@@ -551,51 +612,63 @@
     corner_a, corner_b = pl.pallas_call(
         corner_kernel,
         out_shape=(pltpu.VMEM(corner, f32), pltpu.VMEM((11, prec_y, depth), f32)),
-        in_specs=[vmem_space] * (4 + len(fetched)),
+        in_specs=[vmem_space] * (3 + len(fetched)),
         out_specs=(vmem_space,) * 2,
         compiler_params=params,
         name="corners",
-    )(prec_rel, recv_a, recv_c, recv_d, *fetched)
+    )(prec_rel, recv_c, recv_d, *fetched)
     corner_a = in_vmem(lax.ppermute(corner_a, "gx", swap_pairs(count_x, 0)))
     corner_b = in_vmem(lax.ppermute(corner_b, "gx", swap_pairs(count_x, 1)))
 
-    main_rel, prec_rel = inner(False, "inner_most", main_rel, prec_rel, inlet_a, inlet_b)
-    main_rel, prec_rel = in_vmem(main_rel), in_vmem(prec_rel)
     outs = (
         jax.ShapeDtypeStruct(main_pops.shape, f32),
         jax.ShapeDtypeStruct(prec_pops.shape, f32),
     )
+    stream_scratch = [pltpu.VMEM(main_pops.shape, f32), pltpu.VMEM(prec_pops.shape, f32)]
+    main_rel, main_part, prec_part = pl.pallas_call(
+        middle_kernel,
+        out_shape=(pltpu.VMEM(main_pops.shape, f32), *outs),
+        in_specs=[any_space, vmem_space, any_space] + [vmem_space] * 6,
+        out_specs=(vmem_space, any_space, any_space),
+        scratch_shapes=inner_scratch + stream_scratch
+        + [dma((extent_x,)), dma(()), dma((planes,))],
+        input_output_aliases={3: 0},
+        cost_estimate=long_run,
+        compiler_params=params,
+        name="middle",
+    )(*inner_given, in_vmem(main_rel), prec_rel, recv_c, recv_d, recv_a, inlet)
+    main_rel = in_vmem(main_rel)
     main_part, prec_part = pl.pallas_call(
         stream_kernel,
         out_shape=outs,
-        in_specs=[vmem_space] * 4,
+        in_specs=[vmem_space] * 5 + [any_space] * 2,
         out_specs=(any_space, any_space),
-        scratch_shapes=[
-            pltpu.VMEM(main_pops.shape, f32),
-            pltpu.VMEM(prec_pops.shape, f32),
-            dma((planes,)),
-        ],
+        scratch_shapes=stream_scratch + [dma((planes,))],
+        input_output_aliases={5: 0, 6: 1},
+        cost_estimate=long_run,
         compiler_params=params,
         name="stream",
-        cost_estimate=pl.CostEstimate(flops=10**9, bytes_accessed=1, transcendentals=0),
-    )(main_rel, prec_rel, recv_c, recv_d)
-    main_next, prec_next = pl.pallas_call(
-        edge_kernel,
-        out_shape=outs,
-        in_specs=[vmem_space] * 10 + [any_space] * 2,
-        out_specs=(any_space, any_space),
-        scratch_shapes=[
-            pltpu.VMEM((9, 2, extent_y, depth), f32),
-            pltpu.VMEM((9, 2, prec_y, depth), f32),
-            dma((4,)),
-        ],
-        input_output_aliases={10: 0, 11: 1},
-        compiler_params=params,
-        name="edges",
-    )(
-        main_rel, prec_rel, recv_a, recv_b, recv_c, recv_d,
-        corner_a, corner_b, inlet_a, inlet_b, main_part, prec_part,
-    )
+    )(main_rel, prec_rel, recv_c, recv_d, inlet, main_part, prec_part)
+    def patched(kernel, name, given, outs_so_far):
+        return pl.pallas_call(
+            kernel,
+            out_shape=outs,
+            in_specs=[vmem_space] * len(given) + [any_space] * 2,
+            out_specs=(any_space, any_space),
+            scratch_shapes=[
+                pltpu.VMEM((9, extent_y, depth), f32),
+                pltpu.VMEM((9, prec_y, depth), f32),
+                dma((2,)),
+            ],
+            input_output_aliases={len(given): 0, len(given) + 1: 1},
+            compiler_params=params,
+            name=name,
+        )(*given, *outs_so_far)
+
+    even_given = main_rel, prec_rel, recv_a, corner_a
+    odd_given = main_rel, prec_rel, recv_b, recv_c, recv_d, corner_b, inlet
+    partial = patched(even_edge_kernel, "even_edges", even_given, (main_part, prec_part))
+    main_next, prec_next = patched(odd_edge_kernel, "odd_edges", odd_given, partial)
     return prec_next, main_next
 
 

time: 23.1 us -> 22.8 us (0.987)
  starting transfers between devices: 12.1 us -> 11 us
  Pallas kernels: 8.74 us -> 9.58 us
    ppermute x2 -> x1, starting transfers between devices: 2.57 us -> 1.29 us  [shards(): inlet = in_vmem(lax.ppermute(pair_send, ('gx', 'gy'), to_inlet))]
    pallas_call x5 -> x6, Pallas kernels: 5.59 us -> 6.44 us  [the longest x1 2.35 us: shards(): pl.pallas_call(first_kernel, out_shape=(pltpu.VMEM(main_pops.shape, f32),...]
    ppermute x1, waiting for transfers between devices: 0.01 us -> 0.81 us  [shards(): recv_d = in_vmem(lax.ppermute(send_d, 'gy', swap_pairs(count_y, 1)))]
    ppermute x2 -> x1, waiting for transfers between devices: 0.83 us -> 0.12 us  [shards(): inlet = in_vmem(lax.ppermute(pair_send, ('gx', 'gy'), to_inlet))]
    ppermute x1, starting transfers between devices: 3.54 us -> 3.79 us  [shards(): corner_b = in_vmem(lax.ppermute(corner_b, 'gx', swap_pairs(count_x, 1)))]
  transfers between devices with their start and end apart: 8 -> 7, of which waited for: 2 -> 3; matrix products, arithmetic and copies ran while one was open for 0% -> 0% of each run, Pallas kernels for 21% -> 25%
where the time goes in v4:
time: 22.8 us; the launch traced here: 22.6 us
  starting transfers between devices  11 us (48%)
  Pallas kernels  9.58 us (42%)
  waiting for transfers between devices  1.33 us (6%)
  between operations  0.72 us (3%)
    ppermute x1, starting transfers between devices, shards(): corner_b = in_vmem(lax.ppermute(corner_b, 'gx', swap_pairs(count_x, 1)))  3.79 us
    pallas_call x1, Pallas kernels, shards(): pl.pallas_call(border_kernel, out_shape=(pltpu.VMEM(cell_type.shape, jnp....  3.12 us
    ppermute x1, starting transfers between devices, shards(): recv_a = in_vmem(lax.ppermute(send_a, 'gx', swap_pairs(count_x, 0)))  2.59 us
    pallas_call x1, Pallas kernels, shards(): pl.pallas_call(first_kernel, out_shape=(pltpu.VMEM(main_pops.shape, f32),...  2.35 us
    pallas_call x1, Pallas kernels, shards(): pl.pallas_call(middle_kernel, out_shape=(pltpu.VMEM(main_pops.shape, f32)...  2.34 us
    pallas_call x2, Pallas kernels, patched(): pl.pallas_call(kernel, out_shape=outs, in_specs=[vmem_space] * len(given)...  1.6 us
    ppermute x1, starting transfers between devices, shards(): recv_d = in_vmem(lax.ppermute(send_d, 'gy', swap_pairs(count_y, 1)))  1.33 us
    ppermute x1, starting transfers between devices, shards(): inlet = in_vmem(lax.ppermute(pair_send, ('gx', 'gy'), to_inlet))  1.29 us
  transfers between devices with their start and end apart: 7, of which 3 were waited for; matrix products, arithmetic and copies ran while one was open for 0% of the time, Pallas kernels for 25%

profile of v4, /device:TPU:0, one launch (start us, length us, event | category | flops | bytes accessed | tf_op | source)
XLA Modules:
  0.0 22.6 jit_solution(17944880463006176390)
XLA Ops:
  0.6 3.1 %border.1 = (s32[8,16,256]{2,1,0:T(8,128)S(1)}, f32[27,8,16,256]{3,2,1,0:T(8,128)S(1)}, f32[27,4,8,256]{3,2,1,0:T(8,128)S(1)}, f32[9,24,256]{2,1,0:T(8,128)S(1)}...) custom-call(f32[27,8,16,256]{3,2,1,0:T(8,128)} %main_hbm.5, ...), custom_call_target="tpu_custom_call" | custom-call | tf_op jit(solution)/shard_map/border/pallas_call | solution.py:536
  3.8 0.5 %collective-permute-start = (f32[184,256]{1,0:T(8,128)S(1)}, f32[184,256]{1,0:T(8,128)S(1)}, u32[]{:S(2)}, u32[]{:S(2)}) collective-permute-start(f32[184,256]{1,0:T(8,128)S(1)} %get-tuple-element.29), channel_id=1, source_target_pairs={{0,1},{1,0},{2,3},{3,2},{4,5},{5,4},{6,7},{7,6},{8,9},{9,8},{10,11... | collective-permute-start | bytes 565256 | tf_op jit(solution)/shard_map/ppermute | solution.py:585
  4.3 2.6 %collective-permute-start.2 = (f32[9,24,256]{2,1,0:T(8,128)S(1)}, f32[9,24,256]{2,1,0:T(8,128)S(1)}, u32[]{:S(2)}, u32[]{:S(2)}) collective-permute-start(f32[9,24,256]{2,1,0:T(8,128)S(1)} %get-tuple-element.32), channel_id=1, source_target_pairs={{0,4},{4,0},{8,12},{12,8},{16,20},{20,16},{24,28},{28,24},{1,5},{5... | collective-permute-start | bytes 663560 | tf_op jit(solution)/shard_map/ppermute | solution.py:582
  6.9 0.0 collective-permute-done.recv_c
  6.9 1.3 %collective-permute-start.3 = (f32[2,9,8,256]{3,2,1,0:T(8,128)S(1)}, f32[2,9,8,256]{3,2,1,0:T(8,128)S(1)}, u32[]{:S(2)}, u32[]{:S(2)}) collective-permute-start(f32[2,9,8,256]{3,2,1,0:T(8,128)S(1)} %get-tuple-element.33), channel_id=1, source_target_pairs={{28,0},{29,2},{30,1},{31,3}} | collective-permute-start | bytes 442376 | tf_op jit(solution)/shard_map/ppermute | solution.py:594
  8.2 1.3 %collective-permute-start.1 = (f32[111,256]{1,0:T(8,128)S(1)}, f32[111,256]{1,0:T(8,128)S(1)}, u32[]{:S(2)}, u32[]{:S(2)}) collective-permute-start(f32[111,256]{1,0:T(8,128)S(1)} %get-tuple-element.31), channel_id=1, source_target_pairs={{1,2},{2,1},{3,0},{0,3},{5,6},{6,5},{7,4},{4,7},{9,10},{10,9},{11,... | collective-permute-start | bytes 341000 | tf_op jit(solution)/shard_map/ppermute | solution.py:609
  9.5 2.3 %inner_first.1 = (f32[27,8,16,256]{3,2,1,0:T(8,128)S(1)}, f32[9,16,256]{2,1,0:T(8,128)S(1)}) custom-call(f32[27,8,16,256]{3,2,1,0:T(8,128)} %main_hbm.5, s32[8,16,256]{2,1,0:T(8,128)S(1)} %get-tuple-element.24.cells_in, f32[27]{0:T(128)} %rates_hbm.3, ...), custom_call_target="tpu_custom_call", output_to_operand_aliasing={{0}: (3, {}), {1}: (4, {})} | custom-call | flops 1000000000 | bytes 1 | tf_op jit(solution)/shard_map/inner_first/pallas_call | solution.py:566
  11.9 0.7 %collective-permute-start.4 = (f32[9,16,256]{2,1,0:T(8,128)S(1)}, f32[9,16,256]{2,1,0:T(8,128)S(1)}, u32[]{:S(2)}, u32[]{:S(2)}) collective-permute-start(f32[9,16,256]{2,1,0:T(8,128)S(1)} %get-tuple-element.35), channel_id=1, source_target_pairs={{4,8},{8,4},{12,16},{16,12},{20,24},{24,20},{5,9},{9,5},{13,17},{1... | collective-permute-start | bytes 442376 | tf_op jit(solution)/shard_map/ppermute | solution.py:584
  12.6 0.8 %collective-permute-done.1.recv_d = f32[111,256]{1,0:T(8,128)S(1)} collective-permute-done((f32[111,256]{1,0:T(8,128)S(1)}, f32[111,256]{1,0:T(8,128)S(1)}, u32[]{:S(2)}, u32[]{:S(2)}) %collective-permute-start.1) | collective-permute-done | bytes 113696 | tf_op jit(solution)/shard_map/ppermute | solution.py:609
  13.4 0.8 %collective-permute-start.6 = (f32[2,8,256]{2,1,0:T(8,128)S(1)}, f32[2,8,256]{2,1,0:T(8,128)S(1)}, u32[]{:S(2)}, u32[]{:S(2)}) collective-permute-start(f32[2,8,256]{2,1,0:T(8,128)S(1)} %get-tuple-element.37), channel_id=1, source_target_pairs={{0,4},{4,0},{8,12},{12,8},{16,20},{20,16},{24,28},{28,24},{1,5},{5... | collective-permute-start | bytes 49160 | tf_op jit(solution)/shard_map/ppermute | solution.py:620
  14.2 3.8 %collective-permute-start.5 = (f32[11,8,256]{2,1,0:T(8,128)S(1)}, f32[11,8,256]{2,1,0:T(8,128)S(1)}, u32[]{:S(2)}, u32[]{:S(2)}) collective-permute-start(f32[11,8,256]{2,1,0:T(8,128)S(1)} %get-tuple-element.36), channel_id=1, source_target_pairs={{4,8},{8,4},{12,16},{16,12},{20,24},{24,20},{28,0},{0,28},{5,9},{9... | collective-permute-start | bytes 270344 | tf_op jit(solution)/shard_map/ppermute | solution.py:621
  18.0 0.0 collective-permute-done.2.recv_a
  18.0 0.1 collective-permute-done.3.inlet
  18.1 2.3 %middle.1 = (f32[27,8,16,256]{3,2,1,0:T(8,128)S(1)}, f32[27,8,16,256]{3,2,1,0:T(8,128)}, f32[27,4,8,256]{3,2,1,0:T(8,128)}) custom-call(f32[27,8,16,256]{3,2,1,0:T(8,128)} %main_hbm.5, s32[8,16,256]{2,1,0:T(8,128)S(1)} %get-tuple-element.24.cells_in, f32[27]{0:T(128)} %rates_hbm.3, ...), custom_call_target="tpu_custom_call", output_to_operand_aliasing={{0}: (3, {})} | custom-call | flops 1000000000 | bytes 1 | tf_op jit(solution)/shard_map/middle/pallas_call | solution.py:628
  20.5 0.1 stream.1
  20.6 0.0 collective-permute-done.6.corner_a
  20.6 0.8 %even_edges.1 = (f32[27,8,16,256]{3,2,1,0:T(8,128)}, f32[27,4,8,256]{3,2,1,0:T(8,128)}) custom-call(f32[27,8,16,256]{3,2,1,0:T(8,128)S(1)} %get-tuple-element.34.rel_main, f32[27,4,8,256]{3,2,1,0:T(8,128)S(1)} %get-tuple-element.28.rel_prec, f32[9,24,256]{2,1,0:T(8,128)S(1)} %collective-permute-done.2.recv_a, ...), custom_call_target="tpu_custom_call", output_to_operand_aliasing={{0}: (4, {}), {1}: (5, {})} | custom-call | tf_op jit(solution)/shard_map/even_edges/pallas_call | solution.py:653
  21.4 0.0 collective-permute-done.4.recv_b
  21.4 0.4 %collective-permute-done.5.corner_b = f32[11,8,256]{2,1,0:T(8,128)S(1)} collective-permute-done((f32[11,8,256]{2,1,0:T(8,128)S(1)}, f32[11,8,256]{2,1,0:T(8,128)S(1)}, u32[]{:S(2)}, u32[]{:S(2)}) %collective-permute-start.5) | collective-permute-done | bytes 90144 | tf_op jit(solution)/shard_map/ppermute | solution.py:621
  21.8 0.8 %odd_edges.1 = (f32[27,8,16,256]{3,2,1,0:T(8,128)}, f32[27,4,8,256]{3,2,1,0:T(8,128)}) custom-call(f32[27,8,16,256]{3,2,1,0:T(8,128)S(1)} %get-tuple-element.34.rel_main, f32[27,4,8,256]{3,2,1,0:T(8,128)S(1)} %get-tuple-element.28.rel_prec, f32[9,16,256]{2,1,0:T(8,128)S(1)} %collective-permute-done.4.recv_b, ...), custom_call_target="tpu_custom_call", output_to_operand_aliasing={{0}: (7, {}), {1}: (8, {})} | custom-call | tf_op jit(solution)/shard_map/odd_edges/pallas_call | solution.py:653
  (2 shorter events, 0.1 us)
Async XLA Ops:
  3.8 3.1 %collective-permute-start = (f32[184,256]{1,0:T(8,128)S(1)}, f32[184,256]{1,0:T(8,128)S(1)}, u32[]{:S(2)}, u32[]{:S(2)}) collective-permute-start(f32[184,256]{1,0:T(8,128)S(1)} %get-tuple-element.29), channel_id=1, source_target_pairs={{0,1},{1,0},{2,3},{3,2},{4,5},{5,4},{6,7},{7,6},{8,9},{9,8},{10,11... | collective-permute-start | bytes 565256 | tf_op jit(solution)/shard_map/ppermute | solution.py:585
  4.3 13.7 %collective-permute-start.2 = (f32[9,24,256]{2,1,0:T(8,128)S(1)}, f32[9,24,256]{2,1,0:T(8,128)S(1)}, u32[]{:S(2)}, u32[]{:S(2)}) collective-permute-start(f32[9,24,256]{2,1,0:T(8,128)S(1)} %get-tuple-element.32), channel_id=1, source_target_pairs={{0,4},{4,0},{8,12},{12,8},{16,20},{20,16},{24,28},{28,24},{1,5},{5... | collective-permute-start | bytes 663560 | tf_op jit(solution)/shard_map/ppermute | solution.py:582
  6.9 11.2 %collective-permute-start.3 = (f32[2,9,8,256]{3,2,1,0:T(8,128)S(1)}, f32[2,9,8,256]{3,2,1,0:T(8,128)S(1)}, u32[]{:S(2)}, u32[]{:S(2)}) collective-permute-start(f32[2,9,8,256]{3,2,1,0:T(8,128)S(1)} %get-tuple-element.33), channel_id=1, source_target_pairs={{28,0},{29,2},{30,1},{31,3}} | collective-permute-start | bytes 442376 | tf_op jit(solution)/shard_map/ppermute | solution.py:594
  8.2 5.2 %collective-permute-start.1 = (f32[111,256]{1,0:T(8,128)S(1)}, f32[111,256]{1,0:T(8,128)S(1)}, u32[]{:S(2)}, u32[]{:S(2)}) collective-permute-start(f32[111,256]{1,0:T(8,128)S(1)} %get-tuple-element.31), channel_id=1, source_target_pairs={{1,2},{2,1},{3,0},{0,3},{5,6},{6,5},{7,4},{4,7},{9,10},{10,9},{11,... | collective-permute-start | bytes 341000 | tf_op jit(solution)/shard_map/ppermute | solution.py:609
  11.9 9.6 %collective-permute-start.4 = (f32[9,16,256]{2,1,0:T(8,128)S(1)}, f32[9,16,256]{2,1,0:T(8,128)S(1)}, u32[]{:S(2)}, u32[]{:S(2)}) collective-permute-start(f32[9,16,256]{2,1,0:T(8,128)S(1)} %get-tuple-element.35), channel_id=1, source_target_pairs={{4,8},{8,4},{12,16},{16,12},{20,24},{24,20},{5,9},{9,5},{13,17},{1... | collective-permute-start | bytes 442376 | tf_op jit(solution)/shard_map/ppermute | solution.py:584
  13.4 7.2 %collective-permute-start.6 = (f32[2,8,256]{2,1,0:T(8,128)S(1)}, f32[2,8,256]{2,1,0:T(8,128)S(1)}, u32[]{:S(2)}, u32[]{:S(2)}) collective-permute-start(f32[2,8,256]{2,1,0:T(8,128)S(1)} %get-tuple-element.37), channel_id=1, source_target_pairs={{0,4},{4,0},{8,12},{12,8},{16,20},{20,16},{24,28},{28,24},{1,5},{5... | collective-permute-start | bytes 49160 | tf_op jit(solution)/shard_map/ppermute | solution.py:620
  14.2 7.6 %collective-permute-start.5 = (f32[11,8,256]{2,1,0:T(8,128)S(1)}, f32[11,8,256]{2,1,0:T(8,128)S(1)}, u32[]{:S(2)}, u32[]{:S(2)}) collective-permute-start(f32[11,8,256]{2,1,0:T(8,128)S(1)} %get-tuple-element.36), channel_id=1, source_target_pairs={{4,8},{8,4},{12,16},{16,12},{20,24},{24,20},{28,0},{0,28},{5,9},{9... | collective-permute-start | bytes 270344 | tf_op jit(solution)/shard_map/ppermute | solution.py:621

commit v5 on v4

--- a/solution.py
+++ b/solution.py
@@ -439,85 +439,58 @@
         )
 
 
-def patch_side(low_side, rel_main, rel_prec, faces, out_refs, stages, out_sem):
+def edge_kernel(
+    rel_main, rel_prec, recv_a, recv_b, recv_c, recv_d, corner_a, corner_b, inlet,
+    main_old, prec_old, main_out, prec_out, main_v, prec_v, out_sem,
+):
+    extent_x, extent_y, _ = rel_main.shape[1:]
+    prec_x, prec_y = rel_prec.shape[1:3]
+    planes = extent_x + prec_x
+    place_x, place_y = lax.axis_index("gx"), lax.axis_index("gy")
+    count_x, count_y = lax.axis_size("gx"), lax.axis_size("gy")
+    odd_x = lax.rem(place_x, 2)
+    at_first, at_last = place_x == 0, place_x == count_x - 1
     copies = []
-    for lattice in (1, 0):
-        rel, out_v = (rel_main, rel_prec)[lattice], stages[lattice]
-        x = 0 if low_side else rel.shape[1] - 1
-        first = 18 if low_side else 0
-        for part in range(9):
-            value, halo = faces(lattice, low_side, part)
-            out_v[part] = streamed(part + first, x, rel, value, halo)
-        copies.append(
-            pltpu.make_async_copy(
-                out_v, out_refs[lattice].at[first : first + 9, x], out_sem.at[lattice]
+    for rel, out_v, out_hbm, lattice in (
+        (rel_prec, prec_v, prec_out, 1),
+        (rel_main, main_v, main_out, 0),
+    ):
+        size_x, size_y = rel.shape[1:3]
+        start_y = extent_y if lattice else 0
+        for low_side in (True, False):
+            x = 0 if low_side else size_x - 1
+            from_one = odd_x if low_side else 1 - odd_x
+            for part in range(9):
+                i = part + (18 if low_side else 0)
+                step_y, step_z = digits(i)[1] - 1, digits(i)[2] - 1
+                rows = pl.ds(start_y, size_y)
+                other = corner_b[part] if lattice else recv_b[part]
+                value = jnp.where(from_one == 1, recv_a[part, rows], other)
+                halo = None
+                if step_y:
+                    where = pl.ds((0 if step_y == 1 else 3) + step_z + 1, 1)
+                    halo = jnp.where(
+                        from_one == 1, corner_a[lattice, where, :], corner_b[9 + lattice, where, :]
+                    )
+                if not lattice and low_side:
+                    whole = jnp.concatenate([inlet[0, part], inlet[1, part]], axis=0)
+                    value = jnp.where(at_first, whole, value)
+                if not lattice and not low_side:
+                    value = jnp.where(at_last, rel[i, size_x - 1], value)
+                    if step_y:
+                        row = side_row(recv_c, recv_d, i, size_x - 1, planes)
+                        halo = jnp.where(at_last, row, halo)
+                out_v[part, 0 if low_side else 1] = streamed(i, x, rel, value, halo)
+            first = 18 if low_side else 0
+            copy = pltpu.make_async_copy(
+                out_v.at[:, 0 if low_side else 1],
+                out_hbm.at[first : first + 9, x],
+                out_sem.at[2 * lattice + (0 if low_side else 1)],
             )
-        )
-        copies[-1].start()
+            copy.start()
+            copies.append(copy)
     for copy in copies:
         copy.wait()
-
-
-def face_row(part):
-    step_y, step_z = part // 3 - 1, part % 3 - 1
-    return (0 if step_y == 1 else 3) + step_z + 1 if step_y else None
-
-
-def even_edge_kernel(
-    rel_main, rel_prec, recv_a, corner_a, main_old, prec_old,
-    main_out, prec_out, main_v, prec_v, out_sem,
-):
-    odd_x = lax.rem(lax.axis_index("gx"), 2)
-
-    def faces(lattice, low_side, part):
-        start, size = ((0, main_v.shape[1]), (main_v.shape[1], prec_v.shape[1]))[lattice]
-        row = face_row(part)
-        halo = None if row is None else corner_a[lattice, row : row + 1, :]
-        return recv_a[part, start : start + size], halo
-
-    for low_side in (True, False):
-
-        @pl.when(odd_x == (1 if low_side else 0))
-        def patch(low_side=low_side):
-            patch_side(
-                low_side, rel_main, rel_prec, faces,
-                (main_out, prec_out), (main_v, prec_v), out_sem,
-            )
-
-
-def odd_edge_kernel(
-    rel_main, rel_prec, recv_b, recv_c, recv_d, corner_b, inlet, main_old, prec_old,
-    main_out, prec_out, main_v, prec_v, out_sem,
-):
-    extent_x = rel_main.shape[1]
-    planes = extent_x + rel_prec.shape[1]
-    place_x = lax.axis_index("gx")
-    odd_x = lax.rem(place_x, 2)
-    at_first, at_last = place_x == 0, place_x == lax.axis_size("gx") - 1
-
-    def faces(lattice, low_side, part):
-        row = face_row(part)
-        halo = None if row is None else corner_b[9 + lattice, row : row + 1, :]
-        if lattice:
-            return corner_b[part], halo
-        value = recv_b[part]
-        if low_side:
-            whole = jnp.concatenate([inlet[0, part], inlet[1, part]], axis=0)
-            return jnp.where(at_first, whole, value), halo
-        value = jnp.where(at_last, rel_main[part, extent_x - 1], value)
-        if row is not None:
-            own = side_row(recv_c, recv_d, part, extent_x - 1, planes)
-            halo = jnp.where(at_last, own, halo)
-        return value, halo
-
-    for low_side in (True, False):
-
-        @pl.when(odd_x == (0 if low_side else 1))
-        def patch(low_side=low_side):
-            patch_side(
-                low_side, rel_main, rel_prec, faces,
-                (main_out, prec_out), (main_v, prec_v), out_sem,
-            )
 
 
 def shards(prec_pops, main_pops, cell_type, rates):
@@ -649,26 +622,23 @@
         compiler_params=params,
         name="stream",
     )(main_rel, prec_rel, recv_c, recv_d, inlet, main_part, prec_part)
-    def patched(kernel, name, given, outs_so_far):
-        return pl.pallas_call(
-            kernel,
-            out_shape=outs,
-            in_specs=[vmem_space] * len(given) + [any_space] * 2,
-            out_specs=(any_space, any_space),
-            scratch_shapes=[
-                pltpu.VMEM((9, extent_y, depth), f32),
-                pltpu.VMEM((9, prec_y, depth), f32),
-                dma((2,)),
-            ],
-            input_output_aliases={len(given): 0, len(given) + 1: 1},
-            compiler_params=params,
-            name=name,
-        )(*given, *outs_so_far)
-
-    even_given = main_rel, prec_rel, recv_a, corner_a
-    odd_given = main_rel, prec_rel, recv_b, recv_c, recv_d, corner_b, inlet
-    partial = patched(even_edge_kernel, "even_edges", even_given, (main_part, prec_part))
-    main_next, prec_next = patched(odd_edge_kernel, "odd_edges", odd_given, partial)
+    main_next, prec_next = pl.pallas_call(
+        edge_kernel,
+        out_shape=outs,
+        in_specs=[vmem_space] * 9 + [any_space] * 2,
+        out_specs=(any_space, any_space),
+        scratch_shapes=[
+            pltpu.VMEM((9, 2, extent_y, depth), f32),
+            pltpu.VMEM((9, 2, prec_y, depth), f32),
+            dma((4,)),
+        ],
+        input_output_aliases={9: 0, 10: 1},
+        compiler_params=params,
+        name="edges",
+    )(
+        main_rel, prec_rel, recv_a, recv_b, recv_c, recv_d,
+        corner_a, corner_b, inlet, main_part, prec_part,
+    )
     return prec_next, main_next
 
 

time: 22.8 us -> 23 us (level)
  waiting for transfers between devices: 1.33 us -> 2.15 us
  Pallas kernels: 9.58 us -> 8.88 us
    ppermute x1, waiting for transfers between devices: 0.39 us -> 1.2 us  [shards(): corner_b = in_vmem(lax.ppermute(corner_b, 'gx', swap_pairs(count_x, 1)))]
    pallas_call x2 -> x1, Pallas kernels: 1.6 us -> 0.9 us  [shards(): pl.pallas_call(edge_kernel, out_shape=outs, in_specs=[vmem_space] * 9 + [...]
  transfers between devices with their start and end apart: 7 -> 7, of which waited for: 3 -> 3; matrix products, arithmetic and copies ran while one was open for 0% -> 0% of each run, Pallas kernels for 25% -> 21%
where the time goes in v5:
time: 23 us; the launch traced here: 22.7 us
  starting transfers between devices  11 us (48%)
  Pallas kernels  8.88 us (39%)
  waiting for transfers between devices  2.15 us (9%)
  between operations  0.71 us (3%)
    ppermute x1, starting transfers between devices, shards(): corner_b = in_vmem(lax.ppermute(corner_b, 'gx', swap_pairs(count_x, 1)))  3.79 us
    pallas_call x1, Pallas kernels, shards(): pl.pallas_call(border_kernel, out_shape=(pltpu.VMEM(cell_type.shape, jnp....  3.12 us
    ppermute x1, starting transfers between devices, shards(): recv_a = in_vmem(lax.ppermute(send_a, 'gx', swap_pairs(count_x, 0)))  2.59 us
    pallas_call x1, Pallas kernels, shards(): pl.pallas_call(middle_kernel, out_shape=(pltpu.VMEM(main_pops.shape, f32)...  2.34 us
    pallas_call x1, Pallas kernels, shards(): pl.pallas_call(first_kernel, out_shape=(pltpu.VMEM(main_pops.shape, f32),...  2.33 us
    ppermute x1, starting transfers between devices, shards(): recv_d = in_vmem(lax.ppermute(send_d, 'gy', swap_pairs(count_y, 1)))  1.33 us
    ppermute x1, starting transfers between devices, shards(): inlet = in_vmem(lax.ppermute(pair_send, ('gx', 'gy'), to_inlet))  1.29 us
    ppermute x1, waiting for transfers between devices, shards(): corner_b = in_vmem(lax.ppermute(corner_b, 'gx', swap_pairs(count_x, 1)))  1.2 us
  transfers between devices with their start and end apart: 7, of which 3 were waited for; matrix products, arithmetic and copies ran while one was open for 0% of the time, Pallas kernels for 21%

profile of v5, /device:TPU:0, one launch (start us, length us, event | category | flops | bytes accessed | tf_op | source)
XLA Modules:
  0.0 22.7 jit_solution(6525257234411469993)
XLA Ops:
  0.6 3.1 %border.1 = (s32[8,16,256]{2,1,0:T(8,128)S(1)}, f32[27,8,16,256]{3,2,1,0:T(8,128)S(1)}, f32[27,4,8,256]{3,2,1,0:T(8,128)S(1)}, f32[9,24,256]{2,1,0:T(8,128)S(1)}...) custom-call(f32[27,8,16,256]{3,2,1,0:T(8,128)} %main_hbm.5, ...), custom_call_target="tpu_custom_call" | custom-call | tf_op jit(solution)/shard_map/border/pallas_call | solution.py:509
  3.8 0.5 %collective-permute-start = (f32[184,256]{1,0:T(8,128)S(1)}, f32[184,256]{1,0:T(8,128)S(1)}, u32[]{:S(2)}, u32[]{:S(2)}) collective-permute-start(f32[184,256]{1,0:T(8,128)S(1)} %get-tuple-element.27), channel_id=1, source_target_pairs={{0,1},{1,0},{2,3},{3,2},{4,5},{5,4},{6,7},{7,6},{8,9},{9,8},{10,11... | collective-permute-start | bytes 565256 | tf_op jit(solution)/shard_map/ppermute | solution.py:558
  4.3 2.6 %collective-permute-start.2 = (f32[9,24,256]{2,1,0:T(8,128)S(1)}, f32[9,24,256]{2,1,0:T(8,128)S(1)}, u32[]{:S(2)}, u32[]{:S(2)}) collective-permute-start(f32[9,24,256]{2,1,0:T(8,128)S(1)} %get-tuple-element.30), channel_id=1, source_target_pairs={{0,4},{4,0},{8,12},{12,8},{16,20},{20,16},{24,28},{28,24},{1,5},{5... | collective-permute-start | bytes 663560 | tf_op jit(solution)/shard_map/ppermute | solution.py:555
  6.9 0.0 collective-permute-done.recv_c
  6.9 1.3 %collective-permute-start.3 = (f32[2,9,8,256]{3,2,1,0:T(8,128)S(1)}, f32[2,9,8,256]{3,2,1,0:T(8,128)S(1)}, u32[]{:S(2)}, u32[]{:S(2)}) collective-permute-start(f32[2,9,8,256]{3,2,1,0:T(8,128)S(1)} %get-tuple-element.31), channel_id=1, source_target_pairs={{28,0},{29,2},{30,1},{31,3}} | collective-permute-start | bytes 442376 | tf_op jit(solution)/shard_map/ppermute | solution.py:567
  8.2 1.3 %collective-permute-start.1 = (f32[111,256]{1,0:T(8,128)S(1)}, f32[111,256]{1,0:T(8,128)S(1)}, u32[]{:S(2)}, u32[]{:S(2)}) collective-permute-start(f32[111,256]{1,0:T(8,128)S(1)} %get-tuple-element.29), channel_id=1, source_target_pairs={{1,2},{2,1},{3,0},{0,3},{5,6},{6,5},{7,4},{4,7},{9,10},{10,9},{11,... | collective-permute-start | bytes 341000 | tf_op jit(solution)/shard_map/ppermute | solution.py:582
  9.5 2.3 %inner_first.1 = (f32[27,8,16,256]{3,2,1,0:T(8,128)S(1)}, f32[9,16,256]{2,1,0:T(8,128)S(1)}) custom-call(f32[27,8,16,256]{3,2,1,0:T(8,128)} %main_hbm.5, s32[8,16,256]{2,1,0:T(8,128)S(1)} %get-tuple-element.22.cells_in, f32[27]{0:T(128)} %rates_hbm.3, ...), custom_call_target="tpu_custom_call", output_to_operand_aliasing={{0}: (3, {}), {1}: (4, {})} | custom-call | flops 1000000000 | bytes 1 | tf_op jit(solution)/shard_map/inner_first/pallas_call | solution.py:539
  11.9 0.7 %collective-permute-start.4 = (f32[9,16,256]{2,1,0:T(8,128)S(1)}, f32[9,16,256]{2,1,0:T(8,128)S(1)}, u32[]{:S(2)}, u32[]{:S(2)}) collective-permute-start(f32[9,16,256]{2,1,0:T(8,128)S(1)} %get-tuple-element.33), channel_id=1, source_target_pairs={{4,8},{8,4},{12,16},{16,12},{20,24},{24,20},{5,9},{9,5},{13,17},{1... | collective-permute-start | bytes 442376 | tf_op jit(solution)/shard_map/ppermute | solution.py:557
  12.5 0.8 %collective-permute-done.1.recv_d = f32[111,256]{1,0:T(8,128)S(1)} collective-permute-done((f32[111,256]{1,0:T(8,128)S(1)}, f32[111,256]{1,0:T(8,128)S(1)}, u32[]{:S(2)}, u32[]{:S(2)}) %collective-permute-start.1) | collective-permute-done | bytes 113696 | tf_op jit(solution)/shard_map/ppermute | solution.py:582
  13.4 0.8 %collective-permute-start.5 = (f32[2,8,256]{2,1,0:T(8,128)S(1)}, f32[2,8,256]{2,1,0:T(8,128)S(1)}, u32[]{:S(2)}, u32[]{:S(2)}) collective-permute-start(f32[2,8,256]{2,1,0:T(8,128)S(1)} %get-tuple-element.34), channel_id=1, source_target_pairs={{0,4},{4,0},{8,12},{12,8},{16,20},{20,16},{24,28},{28,24},{1,5},{5... | collective-permute-start | bytes 49160 | tf_op jit(solution)/shard_map/ppermute | solution.py:593
  14.2 3.8 %collective-permute-start.6 = (f32[11,8,256]{2,1,0:T(8,128)S(1)}, f32[11,8,256]{2,1,0:T(8,128)S(1)}, u32[]{:S(2)}, u32[]{:S(2)}) collective-permute-start(f32[11,8,256]{2,1,0:T(8,128)S(1)} %get-tuple-element.35), channel_id=1, source_target_pairs={{4,8},{8,4},{12,16},{16,12},{20,24},{24,20},{28,0},{0,28},{5,9},{9... | collective-permute-start | bytes 270344 | tf_op jit(solution)/shard_map/ppermute | solution.py:594
  18.0 0.0 collective-permute-done.2.recv_a
  18.0 0.1 collective-permute-done.3.inlet
  18.1 2.3 %middle.1 = (f32[27,8,16,256]{3,2,1,0:T(8,128)S(1)}, f32[27,8,16,256]{3,2,1,0:T(8,128)}, f32[27,4,8,256]{3,2,1,0:T(8,128)}) custom-call(f32[27,8,16,256]{3,2,1,0:T(8,128)} %main_hbm.5, s32[8,16,256]{2,1,0:T(8,128)S(1)} %get-tuple-element.22.cells_in, f32[27]{0:T(128)} %rates_hbm.3, ...), custom_call_target="tpu_custom_call", output_to_operand_aliasing={{0}: (3, {})} | custom-call | flops 1000000000 | bytes 1 | tf_op jit(solution)/shard_map/middle/pallas_call | solution.py:601
  20.5 0.1 stream.1
  20.6 0.0 collective-permute-done.4.recv_b
  20.6 0.0 collective-permute-done.5.corner_a
  20.6 1.2 %collective-permute-done.6.corner_b = f32[11,8,256]{2,1,0:T(8,128)S(1)} collective-permute-done((f32[11,8,256]{2,1,0:T(8,128)S(1)}, f32[11,8,256]{2,1,0:T(8,128)S(1)}, u32[]{:S(2)}, u32[]{:S(2)}) %collective-permute-start.6) | collective-permute-done | bytes 90144 | tf_op jit(solution)/shard_map/ppermute | solution.py:594
  21.8 0.9 %edges.1 = (f32[27,8,16,256]{3,2,1,0:T(8,128)}, f32[27,4,8,256]{3,2,1,0:T(8,128)}) custom-call(f32[27,8,16,256]{3,2,1,0:T(8,128)S(1)} %get-tuple-element.32.rel_main, f32[27,4,8,256]{3,2,1,0:T(8,128)S(1)} %get-tuple-element.26.rel_prec, f32[9,24,256]{2,1,0:T(8,128)S(1)} %collective-permute-done.2.recv_a, ...), custom_call_target="tpu_custom_call", output_to_operand_aliasing={{0}: (9, {}), {1}: (10, {})} | custom-call | tf_op jit(solution)/shard_map/edges/pallas_call | solution.py:625
  (2 shorter events, 0.1 us)
Async XLA Ops:
  3.8 3.1 %collective-permute-start = (f32[184,256]{1,0:T(8,128)S(1)}, f32[184,256]{1,0:T(8,128)S(1)}, u32[]{:S(2)}, u32[]{:S(2)}) collective-permute-start(f32[184,256]{1,0:T(8,128)S(1)} %get-tuple-element.27), channel_id=1, source_target_pairs={{0,1},{1,0},{2,3},{3,2},{4,5},{5,4},{6,7},{7,6},{8,9},{9,8},{10,11... | collective-permute-start | bytes 565256 | tf_op jit(solution)/shard_map/ppermute | solution.py:558
  4.3 13.7 %collective-permute-start.2 = (f32[9,24,256]{2,1,0:T(8,128)S(1)}, f32[9,24,256]{2,1,0:T(8,128)S(1)}, u32[]{:S(2)}, u32[]{:S(2)}) collective-permute-start(f32[9,24,256]{2,1,0:T(8,128)S(1)} %get-tuple-element.30), channel_id=1, source_target_pairs={{0,4},{4,0},{8,12},{12,8},{16,20},{20,16},{24,28},{28,24},{1,5},{5... | collective-permute-start | bytes 663560 | tf_op jit(solution)/shard_map/ppermute | solution.py:555
  6.9 11.2 %collective-permute-start.3 = (f32[2,9,8,256]{3,2,1,0:T(8,128)S(1)}, f32[2,9,8,256]{3,2,1,0:T(8,128)S(1)}, u32[]{:S(2)}, u32[]{:S(2)}) collective-permute-start(f32[2,9,8,256]{3,2,1,0:T(8,128)S(1)} %get-tuple-element.31), channel_id=1, source_target_pairs={{28,0},{29,2},{30,1},{31,3}} | collective-permute-start | bytes 442376 | tf_op jit(solution)/shard_map/ppermute | solution.py:567
  8.2 5.2 %collective-permute-start.1 = (f32[111,256]{1,0:T(8,128)S(1)}, f32[111,256]{1,0:T(8,128)S(1)}, u32[]{:S(2)}, u32[]{:S(2)}) collective-permute-start(f32[111,256]{1,0:T(8,128)S(1)} %get-tuple-element.29), channel_id=1, source_target_pairs={{1,2},{2,1},{3,0},{0,3},{5,6},{6,5},{7,4},{4,7},{9,10},{10,9},{11,... | collective-permute-start | bytes 341000 | tf_op jit(solution)/shard_map/ppermute | solution.py:582
  11.9 8.8 %collective-permute-start.4 = (f32[9,16,256]{2,1,0:T(8,128)S(1)}, f32[9,16,256]{2,1,0:T(8,128)S(1)}, u32[]{:S(2)}, u32[]{:S(2)}) collective-permute-start(f32[9,16,256]{2,1,0:T(8,128)S(1)} %get-tuple-element.33), channel_id=1, source_target_pairs={{4,8},{8,4},{12,16},{16,12},{20,24},{24,20},{5,9},{9,5},{13,17},{1... | collective-permute-start | bytes 442376 | tf_op jit(solution)/shard_map/ppermute | solution.py:557
  13.4 7.2 %collective-permute-start.5 = (f32[2,8,256]{2,1,0:T(8,128)S(1)}, f32[2,8,256]{2,1,0:T(8,128)S(1)}, u32[]{:S(2)}, u32[]{:S(2)}) collective-permute-start(f32[2,8,256]{2,1,0:T(8,128)S(1)} %get-tuple-element.34), channel_id=1, source_target_pairs={{0,4},{4,0},{8,12},{12,8},{16,20},{20,16},{24,28},{28,24},{1,5},{5... | collective-permute-start | bytes 49160 | tf_op jit(solution)/shard_map/ppermute | solution.py:593
  14.2 7.6 %collective-permute-start.6 = (f32[11,8,256]{2,1,0:T(8,128)S(1)}, f32[11,8,256]{2,1,0:T(8,128)S(1)}, u32[]{:S(2)}, u32[]{:S(2)}) collective-permute-start(f32[11,8,256]{2,1,0:T(8,128)S(1)} %get-tuple-element.35), channel_id=1, source_target_pairs={{4,8},{8,4},{12,16},{16,12},{20,24},{24,20},{28,0},{0,28},{5,9},{9... | collective-permute-start | bytes 270344 | tf_op jit(solution)/shard_map/ppermute | solution.py:594
